TPU v7x, 128 devices: a whole 4x4x4 slice. The times are simulated.
128 devices in a mesh: ctx: 16 (over y, z), kvh: 8 (over x, core).
Axes of the slice: x: 4, y: 4, z: 4, core: 2. Of those that a mesh axis runs over, the one named last changes fastest.
Arguments:
- queries: bfloat16 [8192, 4096], P('ctx', 'kvh'), may hold values from -113 to 113
- keys: bfloat16 [8192, 1024], P('ctx', 'kvh'), may hold values from -4.5 to 4.5
- values: bfloat16 [8192, 1024], P('ctx', 'kvh'), may hold values from -5 to 5
- span_order: int32 [16], replicated, may hold values from 0 to 15, each once
- ffn_input: bfloat16 [8192, 4096], P('ctx', 'kvh'), may hold values from -6 to 6
- norm_gain: float32 [4096], replicated, may hold values from 0.1 to 1.9
- gate_weight: bfloat16 [4096, 7168], P('ctx', 'kvh'), may hold values from -0.09375 to 0.09375
- up_weight: bfloat16 [4096, 7168], P('ctx', 'kvh'), may hold values from -0.09375 to 0.09375
- down_weight: bfloat16 [7168, 4096], P('kvh', 'ctx'), may hold values from -0.0625 to 0.0625
Outputs:
- attention: bfloat16 [8192, 4096], P('ctx', 'kvh')
- log_sums: float32 [32, 8192], P('kvh', 'ctx')
- ffn_out: bfloat16 [8192, 4096], P('ctx', 'kvh')
Inputs may be any that keep to these rules, and one draw needn't show every extreme that they name: `span_order`: each span number appears once.
All inputs are finite; a program needn't handle non-finite values.
Results may differ from a plain program's by a relative error of at most 0.019.
Values may be sent and summed in bfloat16 or wider, within the bound.
A program may use at most 192 MiB of HBM per device.

v0:
```python
import math

import jax
import jax.numpy as jnp
from jax import lax
from jax.sharding import PartitionSpec as P

H = 32
KVH = 8
HD = 128


def from_behind(x, axis, by):
    length = lax.axis_size(axis)
    return lax.ppermute(x, axis, [(i, (i + by) % length) for i in range(length)])


def body(
    queries, keys, values, span_order, ffn_input, norm_gain, gate_weight, up_weight, down_weight
):
    tok_rows = queries.shape[0]
    local_heads = keys.shape[1] // HD
    group_size = H // KVH
    head_width = queries.shape[1]
    ctx_count = lax.axis_size("ctx")
    device_index = lax.axis_index("ctx")
    span_slots = jnp.arange(ctx_count, dtype=jnp.int32)
    own_span = jnp.sum(jnp.where(span_slots == device_index, span_order, 0))
    offsets = jnp.arange(tok_rows, dtype=jnp.int32)
    query_pos = own_span * tok_rows + offsets
    score_scale = 1.0 / math.sqrt(HD)

    def add_tile(carry_state, row_heads, row_pos, kv_pair, key_pos):
        running_max, running_sum, weighted = carry_state
        key_block = kv_pair[0].reshape(-1, local_heads, HD)
        value_block = kv_pair[1].reshape(-1, local_heads, HD)
        scores = (
            jnp.einsum("qhgd,khd->hgqk", row_heads, key_block, preferred_element_type=jnp.float32)
            * score_scale
        )
        visible = key_pos[None, :] <= row_pos[:, None]
        scores = jnp.where(visible, scores, -1e30)
        new_max = jnp.maximum(running_max, jnp.max(scores, axis=-1))
        factor = jnp.exp(running_max - new_max)
        weights = jnp.where(visible, jnp.exp(scores - new_max[..., None]), 0.0)
        running_sum = running_sum * factor + jnp.sum(weights, axis=-1)
        weighted = weighted * factor[..., None] + jnp.einsum(
            "hgqk,khd->hgqd",
            weights.astype(jnp.bfloat16),
            value_block,
            preferred_element_type=jnp.float32,
        )
        return (new_max, running_sum, weighted)

    def guarded(carry_state, row_heads, row_pos, kv_pair, key_pos):
        return add_tile(carry_state, row_heads, row_pos, kv_pair, key_pos)

    def start_for(count):
        return (
            jnp.full((local_heads, group_size, count), -1e30, jnp.float32),
            jnp.zeros((local_heads, group_size, count), jnp.float32),
            jnp.zeros((local_heads, group_size, count, HD), jnp.float32),
        )

    row_sets = [(queries.reshape(tok_rows, local_heads, group_size, HD), query_pos)]

    def fold_tiles(states, kv_pair, key_pos):
        return tuple(
            (
                guarded(states[slot], row_sets[slot][0], row_sets[slot][1], kv_pair, key_pos)
                for slot in range(len(row_sets))
            )
        )

    start_state = tuple((start_for(row_sets[slot][1].shape[0]) for slot in range(len(row_sets))))
    stacked = jnp.stack([keys, values])
    first_state = fold_tiles(start_state, stacked, query_pos)

    def cycle_turn(turn_index, carry):
        kv_pair, carry_state = carry
        kv_pair = from_behind(kv_pair, "ctx", 1)
        source = (device_index - turn_index) % ctx_count
        key_span = jnp.sum(jnp.where(span_slots == source, span_order, 0))
        return (kv_pair, fold_tiles(carry_state, kv_pair, key_span * tok_rows + offsets))

    final_state = lax.fori_loop(1, ctx_count, cycle_turn, (stacked, first_state))[1]
    running_max, running_sum, weighted = final_state[0]
    count = running_sum.shape[-1]
    rows_out = (
        (weighted / running_sum[..., None])
        .transpose(2, 0, 1, 3)
        .reshape(count, head_width)
        .astype(jnp.bfloat16)
    )
    logs_out = (running_max + jnp.log(running_sum)).reshape(local_heads * group_size, count)
    gathered = lax.all_gather(ffn_input, "kvh", axis=1, tiled=True)
    widened = gathered.astype(jnp.float32)
    mean_sq = jnp.mean(widened * widened, axis=-1, keepdims=True)
    normed = (widened * lax.rsqrt(mean_sq + 1e-05) * norm_gain).astype(jnp.bfloat16)
    gate_sum = jnp.dot(
        normed,
        lax.all_gather(gate_weight, "ctx", axis=0, tiled=True),
        preferred_element_type=jnp.float32,
    )
    up_sum = jnp.dot(
        normed,
        lax.all_gather(up_weight, "ctx", axis=0, tiled=True),
        preferred_element_type=jnp.float32,
    )
    hidden = (jax.nn.silu(gate_sum) * up_sum).astype(jnp.bfloat16)
    partial_terms = jnp.dot(
        hidden,
        lax.all_gather(down_weight, "ctx", axis=1, tiled=True),
        preferred_element_type=jnp.float32,
    )
    ffn_out = lax.psum_scatter(
        partial_terms.astype(jnp.bfloat16), "kvh", scatter_dimension=1, tiled=True
    )
    return (rows_out, logs_out, ffn_out)


def solution(mesh):
    placed = (
        P("ctx", "kvh"),
        P("ctx", "kvh"),
        P("ctx", "kvh"),
        P(),
        P("ctx", "kvh"),
        P(),
        P("ctx", "kvh"),
        P("ctx", "kvh"),
        P("kvh", "ctx"),
    )
    return jax.shard_map(
        body,
        mesh=mesh,
        in_specs=placed,
        out_specs=(P("ctx", "kvh"), P("kvh", "ctx"), P("ctx", "kvh")),
        check_vma=False,
    )
```

profile of v0, /device:TPU:0, one launch (start us, length us, event | category | flops | bytes accessed | tf_op | source)
XLA Modules:
  0.0 496.5 jit_solution(12999621999513711641)
XLA Ops:
  18.4 25.9 %all-gather.5.cloned.1.call-done = bf16[512,4096]{1,0:T(8,128)(2,1)} async-done(((bf16[512,512]{1,0:T(8,128)(2,1)}), bf16[512,4096]{1,0:T(8,128)(2,1)}) %all-gather.5.cloned.1.call-update) | async-done | bytes 4194320 | tf_op jit(solution)/shard_map/all_gather | solution.py:96
  44.3 3.1 fusion.26
  47.4 65.4 %all-gather.7.cloned.1.call-done = bf16[4096,896]{1,0:T(8,128)(2,1)} async-done(((bf16[256,896]{1,0:T(8,128)(2,1)}), bf16[4096,896]{1,0:T(8,128)(2,1)}) %all-gather.7.cloned.1.call-update) | async-done | bytes 7340048 | tf_op jit(solution)/shard_map/all_gather | solution.py:102
  112.7 10.1 %fusion.43 = f32[512,896]{1,0:T(8,128)} fusion(bf16[4096,896]{1,0:T(8,128)(2,1)} %all-gather.7.cloned.1.call-done, bf16[512,4096]{1,0:T(8,128)(2,1)} %all-gather.5.cloned.1.call-done, f32[4096]{0:T(1024)S(1)} %copy-done.3, f32[512]{0:T(512)S(1)} %add_rsqrt_fusion), kind=kOutput, calls=%fused_computation.46 | convolution fusion | flops 3766484992 | bytes 13387776 | tf_op jit(solution)/shard_map/dot_general | solution.py:100
  122.9 64.8 %all-gather.11.cloned.1.call-done = bf16[896,4096]{1,0:T(8,128)(2,1)} async-done(((bf16[896,256]{1,0:T(8,128)(2,1)}), bf16[896,4096]{1,0:T(8,128)(2,1)}) %all-gather.11.cloned.1.call-update) | async-done | bytes 7340048 | tf_op jit(solution)/shard_map/all_gather | solution.py:113
  187.7 67.6 %all-gather.9.cloned.1.call-done = bf16[4096,896]{1,0:T(8,128)(2,1)} async-done(((bf16[256,896]{1,0:T(8,128)(2,1)}), bf16[4096,896]{1,0:T(8,128)(2,1)}) %all-gather.9.cloned.1.call-update) | async-done | bytes 7340048 | tf_op jit(solution)/shard_map/all_gather | solution.py:107
  255.2 16.7 %convolution_convert_fusion = bf16[512,4096]{1,0:T(8,128)(2,1)} fusion(bf16[896,4096]{1,0:T(8,128)(2,1)} %all-gather.11.cloned.1.call-done, f32[512,896]{1,0:T(8,128)} %fusion.43, bf16[4096,896]{1,0:T(8,128)(2,1)} %all-gather.9.cloned.1.call-done, bf16[512,4096]{1,0:T(8,128)(2,1)} %all-gather.5.cloned.1.call-done, f32[4096]{0:T(1024)S(1)} %copy-done.3, ...), kind=kOutput, calls=%fused_computation.34 | convolution fusion | flops 7529431040 | bytes 24922112 | tf_op jit(solution)/shard_map/dot_general | solution.py:111
  272.6 215.1 %while.22 = (s32[]{:T(128)}, bf16[2,512,128]{2,1,0:T(8,128)(2,1)S(1)}, f32[1,4,512]{2,1,0:T(4,128)S(1)}, f32[1,4,512]{2,1,0:T(4,128)S(1)}, f32[1,4,512,128]{3,2,...) while((s32[]{:T(128)}, ...), condition=%wide.region_7.8_spmd.clone, body=%wide.region_3.7_spmd.clone.sunk | while | flops 551296064 | bytes 18227584 | solution.py:86
  275.5 8.5 %collective-permute-done = bf16[2,512,128]{2,1,0:T(8,128)(2,1)S(1)} collective-permute-done((bf16[2,512,128]{2,1,0:T(8,128)(2,1)S(1)}, bf16[2,512,128]{2,1,0:T(8,128)(2,1)S(1)}, u32[]{:S(2)}, u32[]{:S(2)}) %collective-permute-start) | collective-permute-done | bytes 262176 | tf_op jit(solution)/shard_map/while/body/eval_jaxpr/ppermute | solution.py:15
  286.0 1.9 fusion.74
  289.5 8.9 %collective-permute-done = bf16[2,512,128]{2,1,0:T(8,128)(2,1)S(1)} collective-permute-done((bf16[2,512,128]{2,1,0:T(8,128)(2,1)S(1)}, bf16[2,512,128]{2,1,0:T(8,128)(2,1)S(1)}, u32[]{:S(2)}, u32[]{:S(2)}) %collective-permute-start) | collective-permute-done | bytes 262176 | tf_op jit(solution)/shard_map/while/body/eval_jaxpr/ppermute | solution.py:15
  300.5 1.9 fusion.74
  304.0 8.1 %collective-permute-done = bf16[2,512,128]{2,1,0:T(8,128)(2,1)S(1)} collective-permute-done((bf16[2,512,128]{2,1,0:T(8,128)(2,1)S(1)}, bf16[2,512,128]{2,1,0:T(8,128)(2,1)S(1)}, u32[]{:S(2)}, u32[]{:S(2)}) %collective-permute-start) | collective-permute-done | bytes 262176 | tf_op jit(solution)/shard_map/while/body/eval_jaxpr/ppermute | solution.py:15
  314.2 1.9 fusion.74
  317.7 8.1 %collective-permute-done = bf16[2,512,128]{2,1,0:T(8,128)(2,1)S(1)} collective-permute-done((bf16[2,512,128]{2,1,0:T(8,128)(2,1)S(1)}, bf16[2,512,128]{2,1,0:T(8,128)(2,1)S(1)}, u32[]{:S(2)}, u32[]{:S(2)}) %collective-permute-start) | collective-permute-done | bytes 262176 | tf_op jit(solution)/shard_map/while/body/eval_jaxpr/ppermute | solution.py:15
  331.4 8.1 %collective-permute-done = bf16[2,512,128]{2,1,0:T(8,128)(2,1)S(1)} collective-permute-done((bf16[2,512,128]{2,1,0:T(8,128)(2,1)S(1)}, bf16[2,512,128]{2,1,0:T(8,128)(2,1)S(1)}, u32[]{:S(2)}, u32[]{:S(2)}) %collective-permute-start) | collective-permute-done | bytes 262176 | tf_op jit(solution)/shard_map/while/body/eval_jaxpr/ppermute | solution.py:15
  341.6 1.9 fusion.74
  345.1 8.1 %collective-permute-done = bf16[2,512,128]{2,1,0:T(8,128)(2,1)S(1)} collective-permute-done((bf16[2,512,128]{2,1,0:T(8,128)(2,1)S(1)}, bf16[2,512,128]{2,1,0:T(8,128)(2,1)S(1)}, u32[]{:S(2)}, u32[]{:S(2)}) %collective-permute-start) | collective-permute-done | bytes 262176 | tf_op jit(solution)/shard_map/while/body/eval_jaxpr/ppermute | solution.py:15
  355.3 1.9 fusion.74
  358.8 8.1 %collective-permute-done = bf16[2,512,128]{2,1,0:T(8,128)(2,1)S(1)} collective-permute-done((bf16[2,512,128]{2,1,0:T(8,128)(2,1)S(1)}, bf16[2,512,128]{2,1,0:T(8,128)(2,1)S(1)}, u32[]{:S(2)}, u32[]{:S(2)}) %collective-permute-start) | collective-permute-done | bytes 262176 | tf_op jit(solution)/shard_map/while/body/eval_jaxpr/ppermute | solution.py:15
  369.0 1.9 fusion.74
  372.5 8.1 %collective-permute-done = bf16[2,512,128]{2,1,0:T(8,128)(2,1)S(1)} collective-permute-done((bf16[2,512,128]{2,1,0:T(8,128)(2,1)S(1)}, bf16[2,512,128]{2,1,0:T(8,128)(2,1)S(1)}, u32[]{:S(2)}, u32[]{:S(2)}) %collective-permute-start) | collective-permute-done | bytes 262176 | tf_op jit(solution)/shard_map/while/body/eval_jaxpr/ppermute | solution.py:15
  386.2 8.2 %collective-permute-done = bf16[2,512,128]{2,1,0:T(8,128)(2,1)S(1)} collective-permute-done((bf16[2,512,128]{2,1,0:T(8,128)(2,1)S(1)}, bf16[2,512,128]{2,1,0:T(8,128)(2,1)S(1)}, u32[]{:S(2)}, u32[]{:S(2)}) %collective-permute-start) | collective-permute-done | bytes 262176 | tf_op jit(solution)/shard_map/while/body/eval_jaxpr/ppermute | solution.py:15
  399.9 9.3 %collective-permute-done = bf16[2,512,128]{2,1,0:T(8,128)(2,1)S(1)} collective-permute-done((bf16[2,512,128]{2,1,0:T(8,128)(2,1)S(1)}, bf16[2,512,128]{2,1,0:T(8,128)(2,1)S(1)}, u32[]{:S(2)}, u32[]{:S(2)}) %collective-permute-start) | collective-permute-done | bytes 262176 | tf_op jit(solution)/shard_map/while/body/eval_jaxpr/ppermute | solution.py:15
  414.7 10.5 %collective-permute-done = bf16[2,512,128]{2,1,0:T(8,128)(2,1)S(1)} collective-permute-done((bf16[2,512,128]{2,1,0:T(8,128)(2,1)S(1)}, bf16[2,512,128]{2,1,0:T(8,128)(2,1)S(1)}, u32[]{:S(2)}, u32[]{:S(2)}) %collective-permute-start) | collective-permute-done | bytes 262176 | tf_op jit(solution)/shard_map/while/body/eval_jaxpr/ppermute | solution.py:15
  427.2 1.9 fusion.74
  430.8 10.3 %collective-permute-done = bf16[2,512,128]{2,1,0:T(8,128)(2,1)S(1)} collective-permute-done((bf16[2,512,128]{2,1,0:T(8,128)(2,1)S(1)}, bf16[2,512,128]{2,1,0:T(8,128)(2,1)S(1)}, u32[]{:S(2)}, u32[]{:S(2)}) %collective-permute-start) | collective-permute-done | bytes 262176 | tf_op jit(solution)/shard_map/while/body/eval_jaxpr/ppermute | solution.py:15
  443.0 1.9 fusion.74
  446.6 9.5 %collective-permute-done = bf16[2,512,128]{2,1,0:T(8,128)(2,1)S(1)} collective-permute-done((bf16[2,512,128]{2,1,0:T(8,128)(2,1)S(1)}, bf16[2,512,128]{2,1,0:T(8,128)(2,1)S(1)}, u32[]{:S(2)}, u32[]{:S(2)}) %collective-permute-start) | collective-permute-done | bytes 262176 | tf_op jit(solution)/shard_map/while/body/eval_jaxpr/ppermute | solution.py:15
  461.6 8.5 %collective-permute-done = bf16[2,512,128]{2,1,0:T(8,128)(2,1)S(1)} collective-permute-done((bf16[2,512,128]{2,1,0:T(8,128)(2,1)S(1)}, bf16[2,512,128]{2,1,0:T(8,128)(2,1)S(1)}, u32[]{:S(2)}, u32[]{:S(2)}) %collective-permute-start) | collective-permute-done | bytes 262176 | tf_op jit(solution)/shard_map/while/body/eval_jaxpr/ppermute | solution.py:15
  475.7 8.1 %collective-permute-done = bf16[2,512,128]{2,1,0:T(8,128)(2,1)S(1)} collective-permute-done((bf16[2,512,128]{2,1,0:T(8,128)(2,1)S(1)}, bf16[2,512,128]{2,1,0:T(8,128)(2,1)S(1)}, u32[]{:S(2)}, u32[]{:S(2)}) %collective-permute-start) | collective-permute-done | bytes 262176 | tf_op jit(solution)/shard_map/while/body/eval_jaxpr/ppermute | solution.py:15
  485.8 1.9 fusion.74
  (193 shorter events, 69.6 us)
Async XLA Ops:
  7.2 7.6 %copy-start = (bf16[512,512]{1,0:T(8,128)(2,1)S(1)}, bf16[512,512]{1,0:T(8,128)(2,1)}, u32[]{:S(2)}) copy-start(bf16[512,512]{1,0:T(8,128)(2,1)} %param.11) | copy-start | bytes 1572868
  7.2 7.6 %copy-start.1 = (bf16[512,128]{1,0:T(8,128)(2,1)S(1)}, bf16[512,128]{1,0:T(8,128)(2,1)}, u32[]{:S(2)}) copy-start(bf16[512,128]{1,0:T(8,128)(2,1)} %param.12) | copy-start | bytes 393220
  7.2 37.1 %all-gather.5.cloned.1.call-start = ((), (), s32[]{:S(2)}) async-start(), calls=%async_computation.1 | async-start | bytes 4718592 | tf_op jit(solution)/shard_map/all_gather | solution.py:96
  7.9 104.8 %all-gather.7.cloned.1.call-start = ((), (), s32[]{:S(2)}) async-start(), calls=%async_computation.2 | async-start | bytes 7798784 | tf_op jit(solution)/shard_map/all_gather | solution.py:102
  8.7 179.0 %all-gather.11.cloned.1.call-start = ((), (), s32[]{:S(2)}) async-start(), calls=%async_computation.4 | async-start | bytes 7798784 | tf_op jit(solution)/shard_map/all_gather | solution.py:113
  9.4 245.8 %all-gather.9.cloned.1.call-start = ((), (), s32[]{:S(2)}) async-start(), calls=%async_computation.3 | async-start | bytes 7798784 | tf_op jit(solution)/shard_map/all_gather | solution.py:107
  10.0 480.0 %reduce-scatter.2.cloned.1.call-start = ((), (), s32[]{:S(2)}) async-start(), calls=%async_computation.5 | async-start | bytes 4718592 | tf_op jit(solution)/shard_map/reduce_scatter | solution.py:116
  14.8 2.0 copy-start.2
  18.4 94.3 %copy-start.3 = (f32[4096]{0:T(1024)S(1)}, f32[4096]{0:T(1024)}, u32[]{:S(2)}) copy-start(f32[4096]{0:T(1024)} %param.16) | copy-start | bytes 49156
  272.0 0.7 copy-start.4
  272.6 11.4 %collective-permute-start = (bf16[2,512,128]{2,1,0:T(8,128)(2,1)S(1)}, bf16[2,512,128]{2,1,0:T(8,128)(2,1)S(1)}, u32[]{:S(2)}, u32[]{:S(2)}) collective-permute-start(bf16[2,512,128]{2,1,0:T(8,128)(2,1)S(1)} %get-tuple-element.416), channel_id=1, source_target_pairs={{0,8},{8,16},{16,24},{24,32},{32,40},{40,48},{48,56},{56,64},{64,7... | collective-permute-start | bytes 786440 | tf_op jit(solution)/shard_map/while/body/eval_jaxpr/ppermute | solution.py:15
  287.9 10.6 %collective-permute-start = (bf16[2,512,128]{2,1,0:T(8,128)(2,1)S(1)}, bf16[2,512,128]{2,1,0:T(8,128)(2,1)S(1)}, u32[]{:S(2)}, u32[]{:S(2)}) collective-permute-start(bf16[2,512,128]{2,1,0:T(8,128)(2,1)S(1)} %get-tuple-element.416), channel_id=1, source_target_pairs={{0,8},{8,16},{16,24},{24,32},{32,40},{40,48},{48,56},{56,64},{64,7... | collective-permute-start | bytes 786440 | tf_op jit(solution)/shard_map/while/body/eval_jaxpr/ppermute | solution.py:15
  302.4 9.8 %collective-permute-start = (bf16[2,512,128]{2,1,0:T(8,128)(2,1)S(1)}, bf16[2,512,128]{2,1,0:T(8,128)(2,1)S(1)}, u32[]{:S(2)}, u32[]{:S(2)}) collective-permute-start(bf16[2,512,128]{2,1,0:T(8,128)(2,1)S(1)} %get-tuple-element.416), channel_id=1, source_target_pairs={{0,8},{8,16},{16,24},{24,32},{32,40},{40,48},{48,56},{56,64},{64,7... | collective-permute-start | bytes 786440 | tf_op jit(solution)/shard_map/while/body/eval_jaxpr/ppermute | solution.py:15
  316.1 9.8 %collective-permute-start = (bf16[2,512,128]{2,1,0:T(8,128)(2,1)S(1)}, bf16[2,512,128]{2,1,0:T(8,128)(2,1)S(1)}, u32[]{:S(2)}, u32[]{:S(2)}) collective-permute-start(bf16[2,512,128]{2,1,0:T(8,128)(2,1)S(1)} %get-tuple-element.416), channel_id=1, source_target_pairs={{0,8},{8,16},{16,24},{24,32},{32,40},{40,48},{48,56},{56,64},{64,7... | collective-permute-start | bytes 786440 | tf_op jit(solution)/shard_map/while/body/eval_jaxpr/ppermute | solution.py:15
  329.8 9.8 %collective-permute-start = (bf16[2,512,128]{2,1,0:T(8,128)(2,1)S(1)}, bf16[2,512,128]{2,1,0:T(8,128)(2,1)S(1)}, u32[]{:S(2)}, u32[]{:S(2)}) collective-permute-start(bf16[2,512,128]{2,1,0:T(8,128)(2,1)S(1)} %get-tuple-element.416), channel_id=1, source_target_pairs={{0,8},{8,16},{16,24},{24,32},{32,40},{40,48},{48,56},{56,64},{64,7... | collective-permute-start | bytes 786440 | tf_op jit(solution)/shard_map/while/body/eval_jaxpr/ppermute | solution.py:15
  343.5 9.8 %collective-permute-start = (bf16[2,512,128]{2,1,0:T(8,128)(2,1)S(1)}, bf16[2,512,128]{2,1,0:T(8,128)(2,1)S(1)}, u32[]{:S(2)}, u32[]{:S(2)}) collective-permute-start(bf16[2,512,128]{2,1,0:T(8,128)(2,1)S(1)} %get-tuple-element.416), channel_id=1, source_target_pairs={{0,8},{8,16},{16,24},{24,32},{32,40},{40,48},{48,56},{56,64},{64,7... | collective-permute-start | bytes 786440 | tf_op jit(solution)/shard_map/while/body/eval_jaxpr/ppermute | solution.py:15
  357.2 9.8 %collective-permute-start = (bf16[2,512,128]{2,1,0:T(8,128)(2,1)S(1)}, bf16[2,512,128]{2,1,0:T(8,128)(2,1)S(1)}, u32[]{:S(2)}, u32[]{:S(2)}) collective-permute-start(bf16[2,512,128]{2,1,0:T(8,128)(2,1)S(1)} %get-tuple-element.416), channel_id=1, source_target_pairs={{0,8},{8,16},{16,24},{24,32},{32,40},{40,48},{48,56},{56,64},{64,7... | collective-permute-start | bytes 786440 | tf_op jit(solution)/shard_map/while/body/eval_jaxpr/ppermute | solution.py:15
  370.9 9.8 %collective-permute-start = (bf16[2,512,128]{2,1,0:T(8,128)(2,1)S(1)}, bf16[2,512,128]{2,1,0:T(8,128)(2,1)S(1)}, u32[]{:S(2)}, u32[]{:S(2)}) collective-permute-start(bf16[2,512,128]{2,1,0:T(8,128)(2,1)S(1)} %get-tuple-element.416), channel_id=1, source_target_pairs={{0,8},{8,16},{16,24},{24,32},{32,40},{40,48},{48,56},{56,64},{64,7... | collective-permute-start | bytes 786440 | tf_op jit(solution)/shard_map/while/body/eval_jaxpr/ppermute | solution.py:15
  384.6 9.8 %collective-permute-start = (bf16[2,512,128]{2,1,0:T(8,128)(2,1)S(1)}, bf16[2,512,128]{2,1,0:T(8,128)(2,1)S(1)}, u32[]{:S(2)}, u32[]{:S(2)}) collective-permute-start(bf16[2,512,128]{2,1,0:T(8,128)(2,1)S(1)} %get-tuple-element.416), channel_id=1, source_target_pairs={{0,8},{8,16},{16,24},{24,32},{32,40},{40,48},{48,56},{56,64},{64,7... | collective-permute-start | bytes 786440 | tf_op jit(solution)/shard_map/while/body/eval_jaxpr/ppermute | solution.py:15
  398.3 10.9 %collective-permute-start = (bf16[2,512,128]{2,1,0:T(8,128)(2,1)S(1)}, bf16[2,512,128]{2,1,0:T(8,128)(2,1)S(1)}, u32[]{:S(2)}, u32[]{:S(2)}) collective-permute-start(bf16[2,512,128]{2,1,0:T(8,128)(2,1)S(1)} %get-tuple-element.416), channel_id=1, source_target_pairs={{0,8},{8,16},{16,24},{24,32},{32,40},{40,48},{48,56},{56,64},{64,7... | collective-permute-start | bytes 786440 | tf_op jit(solution)/shard_map/while/body/eval_jaxpr/ppermute | solution.py:15
  413.1 12.1 %collective-permute-start = (bf16[2,512,128]{2,1,0:T(8,128)(2,1)S(1)}, bf16[2,512,128]{2,1,0:T(8,128)(2,1)S(1)}, u32[]{:S(2)}, u32[]{:S(2)}) collective-permute-start(bf16[2,512,128]{2,1,0:T(8,128)(2,1)S(1)} %get-tuple-element.416), channel_id=1, source_target_pairs={{0,8},{8,16},{16,24},{24,32},{32,40},{40,48},{48,56},{56,64},{64,7... | collective-permute-start | bytes 786440 | tf_op jit(solution)/shard_map/while/body/eval_jaxpr/ppermute | solution.py:15
  429.1 11.9 %collective-permute-start = (bf16[2,512,128]{2,1,0:T(8,128)(2,1)S(1)}, bf16[2,512,128]{2,1,0:T(8,128)(2,1)S(1)}, u32[]{:S(2)}, u32[]{:S(2)}) collective-permute-start(bf16[2,512,128]{2,1,0:T(8,128)(2,1)S(1)} %get-tuple-element.416), channel_id=1, source_target_pairs={{0,8},{8,16},{16,24},{24,32},{32,40},{40,48},{48,56},{56,64},{64,7... | collective-permute-start | bytes 786440 | tf_op jit(solution)/shard_map/while/body/eval_jaxpr/ppermute | solution.py:15
  445.0 11.1 %collective-permute-start = (bf16[2,512,128]{2,1,0:T(8,128)(2,1)S(1)}, bf16[2,512,128]{2,1,0:T(8,128)(2,1)S(1)}, u32[]{:S(2)}, u32[]{:S(2)}) collective-permute-start(bf16[2,512,128]{2,1,0:T(8,128)(2,1)S(1)} %get-tuple-element.416), channel_id=1, source_target_pairs={{0,8},{8,16},{16,24},{24,32},{32,40},{40,48},{48,56},{56,64},{64,7... | collective-permute-start | bytes 786440 | tf_op jit(solution)/shard_map/while/body/eval_jaxpr/ppermute | solution.py:15
  460.0 10.2 %collective-permute-start = (bf16[2,512,128]{2,1,0:T(8,128)(2,1)S(1)}, bf16[2,512,128]{2,1,0:T(8,128)(2,1)S(1)}, u32[]{:S(2)}, u32[]{:S(2)}) collective-permute-start(bf16[2,512,128]{2,1,0:T(8,128)(2,1)S(1)} %get-tuple-element.416), channel_id=1, source_target_pairs={{0,8},{8,16},{16,24},{24,32},{32,40},{40,48},{48,56},{56,64},{64,7... | collective-permute-start | bytes 786440 | tf_op jit(solution)/shard_map/while/body/eval_jaxpr/ppermute | solution.py:15
  474.1 9.8 %collective-permute-start = (bf16[2,512,128]{2,1,0:T(8,128)(2,1)S(1)}, bf16[2,512,128]{2,1,0:T(8,128)(2,1)S(1)}, u32[]{:S(2)}, u32[]{:S(2)}) collective-permute-start(bf16[2,512,128]{2,1,0:T(8,128)(2,1)S(1)} %get-tuple-element.416), channel_id=1, source_target_pairs={{0,8},{8,16},{16,24},{24,32},{32,40},{40,48},{48,56},{56,64},{64,7... | collective-permute-start | bytes 786440 | tf_op jit(solution)/shard_map/while/body/eval_jaxpr/ppermute | solution.py:15
Sparse Core Ops, SparseCore 0:
  9.7 34.5 all-gather.4
  46.5 66.2 all-gather.6
  114.9 72.7 all-gather.10
  189.7 65.4 all-gather.8
  272.1 37.5 reduce-scatter.1
where the time goes:
time: 497 us
  waiting for transfers between devices  357 us (72%)
  matrix products  71.1 us (14%)
  other arithmetic  36.7 us (7%)
  between operations  14.6 us (3%)
  loops' own time  10.9 us (2%)
    ppermute x15, waiting for transfers between devices, from_behind(): lax.ppermute(x, axis, [(i, (i + by) % length) for i in range(length)])  131 us
    all_gather x1, waiting for transfers between devices, body(): lax.all_gather(up_weight, 'ctx', axis=0, tiled=True)  67.6 us
    all_gather x1, waiting for transfers between devices, body(): lax.all_gather(gate_weight, 'ctx', axis=0, tiled=True)  65.4 us
    all_gather x1, waiting for transfers between devices, body(): lax.all_gather(down_weight, 'ctx', axis=1, tiled=True)  64.8 us
    dot_general x16, matrix products, add_tile(): jnp.einsum('hgqk,khd->hgqd', weights.astype(jnp.bfloat16), value_block, p...  30.3 us
    all_gather x1, waiting for transfers between devices, body(): gathered = lax.all_gather(ffn_input, 'kvh', axis=1, tiled=True)  25.9 us
    dot_general x1, matrix products, body(): jnp.dot(hidden, lax.all_gather(down_weight, 'ctx', axis=1, tiled=True), p...  16.7 us
    reduce_sum x16, other arithmetic, add_tile(): running_sum = running_sum * factor + jnp.sum(weights, axis=-1)  16.7 us
  transfers between devices with their start and end apart: 20, of which 19 were waited for; matrix products, arithmetic and copies ran while one was open for 19% of the time, Pallas kernels for 0%

commit v1 on v0

v1 whole, which is shorter than its diff:
```python
import functools
import math

import jax
import jax.numpy as jnp
from jax import lax
from jax.experimental import pallas as pl
from jax.experimental.pallas import tpu as pltpu
from jax.sharding import PartitionSpec as P

MESH = pl.DeviceIdType.MESH
HD = 128
TOK = 512
BF = jnp.bfloat16
F32 = jnp.float32
KV, GATE, UP, DOWN = range(4)
LOG2E = math.log2(math.e)
SCALE2 = LOG2E / math.sqrt(HD)


def kernel(
    span_ref, gain_ref, q_in, kv_in, f_in, g_in, u_in, d_in,
    att_out, log_out, ffn_out,
    kv_b, g_b, u_b, d_b,
    q_b, f_b, n_b, m_b, acc_b, o_b, orx_b, lg_b, lrx_b,
    ga_b, ua_b, hid_b, ps_b, po_b, rs_b, r_b, rx_b, fs_b, fo_b,
    loc_sem, send_sem, recv_sem, xs_sem, xr_sem,
):
    ctx = lax.axis_index("ctx")
    kvh = lax.axis_index("kvh")
    x, c = kvh // 2, kvh % 2
    y, z = ctx // 4, ctx % 4
    h = y // 2
    same = c * h + (1 - c) * (1 - h)
    is_same = c == h
    not_same = c != h
    yp = y + 1 - 2 * (y % 2)
    yo = 3 - y
    yq = (y + 2) % 4
    yt = same * y + (1 - same) * yo

    def dev(xx, yy, zz, cc):
        return {"ctx": yy * 4 + zz, "kvh": xx * 2 + cc}

    zr, zl, zf = (z + 1) % 4, (z + 3) % 4, (z + 2) % 4
    xr, xl, xf = (x + 1) % 4, (x + 3) % 4, (x + 2) % 4
    SIB = dev(x, y, z, 1 - c)
    PART = dev(x, yp, z, c)
    OPP = dev(x, yo, z, c)
    OPPD = dev(x, yo, z, 1 - c)
    ZR, ZL = dev(x, y, zr, c), dev(x, y, zl, c)
    XR, XL, XF = dev(xr, y, z, c), dev(xl, y, z, c), dev(xf, y, z, c)

    barrier = pltpu.get_barrier_semaphore()
    for t in (SIB, PART, OPP, OPPD, ZR, ZL, XR, XL, XF):
        pl.semaphore_signal(barrier, inc=1, device_id=t, device_id_type=MESH)
    pl.semaphore_wait(barrier, 9)

    sent = []

    def remote(src, dst, ss, rs, target):
        return pltpu.make_async_remote_copy(
            src_ref=src, dst_ref=dst, send_sem=ss, recv_sem=rs,
            device_id=target, device_id_type=MESH,
        )

    bufs = (kv_b, g_b, u_b, d_b)
    ins = (kv_in, g_in, u_in, d_in)
    own = 4 * z + y
    slot_c = same * own + (1 - same) * 16
    yb = (y, yp, yo, yq)
    cps = {}

    def send(a, idx, src, dst, target, go=True):
        cp = remote(src, dst, send_sem.at[a, idx], recv_sem.at[a, idx], target)
        cps[a, idx] = cp
        if go:
            cp.start()
            sent.append(cp)
        return cp

    def block(a, s):
        return bufs[a].at[s, c]

    def pair(a, s):
        return bufs[a].at[pl.ds(s, 2), c]

    def quad(a, s):
        return bufs[a].at[pl.ds(s, 4), c]

    locs = {}

    def start0(a):
        cp = pltpu.make_async_copy(ins[a].at[c], bufs[a].at[slot_c, c], loc_sem.at[a])
        cp.start()
        locs[a] = cp
        send(a, 0, ins[a].at[1 - c], bufs[a].at[slot_c, 1 - c], SIB)

    P0 = 2 * h
    P1 = 2 - 2 * h

    def z_sends(a, b):
        s = 4 * z + yb[b]
        send(a, 4 + b, block(a, s), block(a, s), ZR)
        send(a, 8 + b, block(a, s), block(a, s), ZL)

    def ev(a, n):
        if n == 0:
            locs[a].wait()
            cps[a, 0].wait_recv()
            send(a, 1, block(a, own), block(a, own), PART)
            send(a, 2, block(a, 16), block(a, own), OPP)
            z_sends(a, 0)
        elif n == 1:
            cps[a, 1].wait_recv()
            z_sends(a, 1)
        elif n == 2:
            cps[a, 2].wait_recv()
            s = 4 * z + yo
            send(a, 3, block(a, s), block(a, s), PART)
            z_sends(a, 2)
        elif n == 3:
            cps[a, 3].wait_recv()
            z_sends(a, 3)
            send(a, 14, quad(a, 4 * z), quad(a, 4 * z), SIB)
        elif n == 4:
            cps[a, 4].wait_recv()
            cps[a, 5].wait_recv()
            s = 4 * zl + P0
            send(a, 12, pair(a, s), pair(a, s), ZR)
        elif n == 5:
            cps[a, 10].wait_recv()
            cps[a, 11].wait_recv()
            s = 4 * zr + P1
            send(a, 13, pair(a, s), pair(a, s), ZL)
        elif n == 6:
            cps[a, 6].wait_recv()
            cps[a, 7].wait_recv()
            send(a, 15, quad(a, 4 * zl), quad(a, 4 * zl), SIB)
            cps[a, 8].wait_recv()
            cps[a, 9].wait_recv()
            send(a, 16, quad(a, 4 * zr), quad(a, 4 * zr), SIB)
        elif n == 7:
            cps[a, 12].wait_recv()
            cps[a, 13].wait_recv()
            send(a, 17, quad(a, 4 * zf), quad(a, 4 * zf), SIB)

    def xs(i, src, dst, target):
        return remote(src, dst, xs_sem.at[i], xr_sem.at[i], target)

    k0 = 2 * x + c
    f_loc = pltpu.make_async_copy(f_in, f_b.at[k0], loc_sem.at[4])
    f_sib = xs(0, f_in, f_b.at[k0], SIB)
    f_opp_same = remote(f_in, f_b.at[k0], xs_sem.at[1], xr_sem.at[1 + c], OPP)
    f_opp_diag = remote(f_in, f_b.at[k0], xs_sem.at[1], xr_sem.at[1 + c], OPPD)
    q_loc = pltpu.make_async_copy(q_in, q_b, loc_sem.at[5])
    q_swap = xs(3, q_in, q_b, OPPD)

    @pl.when(is_same)
    def _():
        q_loc.start()
        f_loc.start()
        f_opp_same.start()

    @pl.when(not_same)
    def _():
        q_swap.start()
        f_sib.start()
        f_opp_diag.start()

    def f_wait():
        @pl.when(is_same)
        def _():
            f_loc.wait()
            f_sib.wait_recv()
            f_opp_same.wait_send()

        @pl.when(not_same)
        def _():
            for j in range(2):
                remote(f_in, f_b.at[0], xs_sem.at[1], xr_sem.at[1 + j], OPPD).wait_recv()
            f_opp_diag.wait_send()
            f_sib.wait_send()

    def q_wait():
        @pl.when(is_same)
        def _():
            q_loc.wait()

        @pl.when(not_same)
        def _():
            q_swap.wait()

    fx = {}

    def fev(n):
        if n == 0:
            f_wait()
            mine = f_b.at[pl.ds(2 * x, 2)]
            for i, t in ((4, XR), (5, XL)):
                fx[i] = xs(i, mine, mine, t)
                fx[i].start()
                sent.append(fx[i])
        elif n == 1:
            fx[4].wait_recv()
            one = f_b.at[2 * xl]
            fx[6] = xs(6, one, one, XR)
            fx[6].start()
            sent.append(fx[6])
        elif n == 2:
            fx[5].wait_recv()
            one = f_b.at[2 * xr + 1]
            fx[7] = xs(7, one, one, XL)
            fx[7].start()
            sent.append(fx[7])
        elif n == 3:
            fx[6].wait_recv()
            fx[7].wait_recv()

    events = []

    def add(*names):
        for nm in names:
            a, n = nm[0], int(nm[1:])
            if a == "F":
                events.append((nm, functools.partial(fev, n)))
            else:
                events.append((nm, functools.partial(ev, "KGUD".index(a), n)))

    add("K0", "F0", "G0", "K1", "K2", "K3", "G1", "K4", "K5", "G2", "K6", "G3", "U0", "K7")
    add("U1", "G4", "F1", "U2", "G5", "F2", "U3", "G6", "F3", "D0", "G7", "U4", "U5", "U6")
    add("D1", "D2", "D3", "U7", "D4", "D5", "D6", "D7")
    done = set()
    at = [0]

    def pump(count):
        for _ in range(count):
            if at[0] < len(events):
                nm, fn = events[at[0]]
                fn()
                done.add(nm)
                at[0] += 1

    def until(nm):
        while nm not in done:
            pump(1)

    groups = (z, zl, zr, zf)
    ready = ("3", "6", "6", "7")

    def group_ready(a, i):
        until("KGUD"[a] + ready[i])
        cps[a, 14 + i].wait_recv()

    start0(KV)
    start0(GATE)
    start0(UP)
    start0(DOWN)

    my_span = span_ref[yt * 4 + z]

    def attend(slot, src, first):
        visible = (span_ref[src] < my_span).astype(F32)
        hide = (1.0 - visible) * 1e30

        def head(g, _):
            k = kv_b[slot, 0]
            v = kv_b[slot, 1]
            va = jnp.concatenate([v, jnp.ones((TOK, HD), BF)], axis=1)
            col = pl.multiple_of(g * HD, HD)
            for t in range(2):
                rows = pl.ds(t * 256, 256)
                q = q_b[rows, pl.ds(col, HD)]
                s = lax.dot_general(q, k, (((1,), (1,)), ((), ())), preferred_element_type=F32)
                if first:
                    ri = lax.broadcasted_iota(jnp.int32, (256, TOK), 0) + t * 256
                    ci = lax.broadcasted_iota(jnp.int32, (256, TOK), 1)
                    s = jnp.where(ci <= ri, s, -1e30)
                    top = jnp.broadcast_to(jnp.max(s, axis=1, keepdims=True), (256, HD))
                    m_new = top * SCALE2
                    p = jnp.exp2(s * SCALE2 - jnp.concatenate([m_new] * 4, axis=1))
                    acc_b[g, rows] = jnp.dot(p.astype(BF), va, preferred_element_type=F32)
                else:
                    top = jnp.broadcast_to(jnp.max(s, axis=1, keepdims=True), (256, HD))
                    m_old = m_b[g, rows]
                    m_new = jnp.maximum(m_old, top * SCALE2 - hide)
                    alpha = jnp.exp2(m_old - m_new)
                    sub = m_new + hide
                    p = jnp.exp2(s * SCALE2 - jnp.concatenate([sub] * 4, axis=1))
                    pv = jnp.dot(p.astype(BF), va, preferred_element_type=F32)
                    acc_b[g, rows] = acc_b[g, rows] * jnp.concatenate([alpha] * 2, axis=1) + pv
                m_b[g, rows] = m_new
            return 0

        lax.fori_loop(0, 4, head, 0)

    def attend_group(i, pumps):
        group_ready(KV, i)
        zs = groups[i]
        for j in range(4):
            ys = (yt + j) % 4
            attend(4 * zs + ys, ys * 4 + zs, i == 0 and j == 0)
            pump(pumps)

    until("K3")
    q_wait()
    attend_group(0, 1)
    attend_group(1, 1)
    attend_group(2, 1)
    attend_group(3, 1)

    def finish(g, _):
        col = pl.multiple_of(g * HD, HD)
        total = acc_b[g, :, HD:]
        o_b[:, pl.ds(col, HD)] = (acc_b[g, :, :HD] / total).astype(BF)
        logs = m_b[g] * (1.0 / LOG2E) + jnp.log(total)
        lg_b[g] = jnp.transpose(logs)[:8]
        return 0

    lax.fori_loop(0, 4, finish, 0)
    o_swap = xs(8, o_b, orx_b, OPPD)
    l_swap = xs(9, lg_b, lrx_b, OPPD)

    @pl.when(is_same)
    def _():
        att_out[...] = o_b[...]
        for g in range(4):
            log_out[pl.ds(g, 1)] = lg_b[g, :1]

    @pl.when(not_same)
    def _():
        o_swap.start()
        l_swap.start()

    until("F3")

    def norm(i, _):
        rows = pl.ds(i * 64, 64)
        part = jnp.zeros((64, TOK), F32)
        for k in range(8):
            v = f_b[k, rows].astype(F32)
            part = part + v * v
        r = lax.rsqrt(jnp.sum(part, axis=1, keepdims=True) * (1.0 / 4096) + 1e-05)
        for k in range(8):
            n_b[k, rows] = (f_b[k, rows].astype(F32) * r * gain_ref[pl.ds(k, 1)]).astype(BF)
        return 0

    lax.fori_loop(0, 8, norm, 0)

    def project(a, i):
        group_ready(a, i)
        zs = groups[i]
        out = ga_b if a == GATE else ua_b
        off = pl.multiple_of((zs % 2) * 256, 256)

        def rows_of(t, _):
            rows = pl.ds(t * 256, 256)
            lhs = jnp.concatenate(
                [n_b[2 * ys + zs // 2, rows, pl.ds(off, 256)] for ys in range(4)], axis=1
            )
            w = bufs[a][pl.ds(4 * zs, 4)].reshape(1024, 896)
            res = jnp.dot(lhs, w, preferred_element_type=F32)
            if i == 0:
                out[rows] = res
            else:
                out[rows] = out[rows] + res
            return 0

        lax.fori_loop(0, 2, rows_of, 0)

    for i in range(4):
        project(GATE, i)
    for i in range(4):
        project(UP, i)

    def act(i, _):
        rows = pl.ds(i * 64, 64)
        g = ga_b[rows]
        hid_b[rows] = (g / (1.0 + jnp.exp(-g)) * ua_b[rows]).astype(BF)
        return 0

    lax.fori_loop(0, 8, act, 0)

    rel = ((2, xf, XF), (0, xr, XR), (1, xl, XL))
    rsc = {}

    def down(i):
        group_ready(DOWN, i)
        zs = groups[i]
        for n, xd, target in rel:
            w = d_b[4 * zs + xd].reshape(896, 256)
            ps_b[i, n] = jnp.dot(hid_b[...], w, preferred_element_type=F32).astype(BF)
            cp = xs(10 + 3 * i + n, ps_b.at[i, n], rs_b.at[i, n], target)
            cp.start()
            sent.append(cp)
            rsc[i, n] = cp
        w = d_b[4 * zs + x].reshape(896, 256)
        po_b[i] = jnp.dot(hid_b[...], w, preferred_element_type=F32)

    tail = []

    def combine(i):
        zs = groups[i]
        for n in range(3):
            rsc[i, n].wait_recv()
        to_opp = xs(22 + i, r_b.at[i], rx_b.at[i], OPP)
        total = po_b[i]
        for n in range(3):
            total = total + rs_b[i, n].astype(F32)
        po_b[i] = total

        @pl.when(not_same)
        def _():
            r_b[i] = po_b[i].astype(BF)
            to_opp.start()

        tail.append(to_opp)

    def close(i):
        zs = groups[i]
        sub = zs % 2
        here = zs // 2 == c
        off = pl.multiple_of(sub * 256, 256)
        to_sib = remote(fs_b.at[i], fo_b.at[sub], xs_sem.at[26 + i], xr_sem.at[26 + sub], SIB)

        @pl.when(is_same)
        def _():
            tail[i].wait_recv()
            res = (po_b[i] + rx_b[i].astype(F32)).astype(BF)

            @pl.when(here)
            def _():
                ffn_out[:, pl.ds(off, 256)] = res

            @pl.when(zs // 2 != c)
            def _():
                fs_b[i] = res
                to_sib.start()

        return to_sib

    sibs = []
    down(0)
    down(1)
    combine(0)
    down(2)
    combine(1)
    sibs.append(close(0))
    down(3)
    combine(2)
    sibs.append(close(1))
    combine(3)
    sibs.append(close(2))
    sibs.append(close(3))

    @pl.when(is_same)
    def _():
        for i in range(4):
            @pl.when(groups[i] // 2 != c)
            def _():
                sibs[i].wait_send()

    @pl.when(not_same)
    def _():
        o_swap.wait()
        l_swap.wait()
        att_out[...] = orx_b[...]
        for g in range(4):
            log_out[pl.ds(g, 1)] = lrx_b[g, :1]
        for i in range(4):
            tail[i].wait_send()
        for s in range(2):
            remote(fs_b.at[0], fo_b.at[s], xs_sem.at[26], xr_sem.at[26 + s], SIB).wait_recv()
            ffn_out[:, s * 256 : (s + 1) * 256] = fo_b[s]

    for cp in sent:
        cp.wait_send()


def body(queries, keys, values, span_order, ffn_input, norm_gain, gate_w, up_w, down_w):
    anyspace = pl.BlockSpec(memory_space=pl.ANY)
    vmem = pl.BlockSpec(memory_space=pltpu.VMEM)
    smem = pl.BlockSpec(memory_space=pltpu.SMEM)
    sem = pltpu.SemaphoreType.DMA
    return pl.pallas_call(
        kernel,
        out_shape=(
            jax.ShapeDtypeStruct((512, 512), BF),
            jax.ShapeDtypeStruct((4, 512), F32),
            jax.ShapeDtypeStruct((512, 512), BF),
        ),
        in_specs=[smem, vmem] + [anyspace] * 6,
        out_specs=(vmem, vmem, vmem),
        scratch_shapes=[
            pltpu.VMEM((17, 2, 512, 128), BF),
            pltpu.VMEM((17, 2, 128, 896), BF),
            pltpu.VMEM((17, 2, 128, 896), BF),
            pltpu.VMEM((17, 2, 448, 256), BF),
            pltpu.VMEM((512, 512), BF),
            pltpu.VMEM((8, 512, 512), BF),
            pltpu.VMEM((8, 512, 512), BF),
            pltpu.VMEM((4, 512, 128), F32),
            pltpu.VMEM((4, 512, 256), F32),
            pltpu.VMEM((512, 512), BF),
            pltpu.VMEM((512, 512), BF),
            pltpu.VMEM((4, 8, 512), F32),
            pltpu.VMEM((4, 8, 512), F32),
            pltpu.VMEM((512, 896), F32),
            pltpu.VMEM((512, 896), F32),
            pltpu.VMEM((512, 896), BF),
            pltpu.VMEM((4, 3, 512, 256), BF),
            pltpu.VMEM((4, 512, 256), F32),
            pltpu.VMEM((4, 3, 512, 256), BF),
            pltpu.VMEM((4, 512, 256), BF),
            pltpu.VMEM((4, 512, 256), BF),
            pltpu.VMEM((4, 512, 256), BF),
            pltpu.VMEM((2, 512, 256), BF),
            sem((6,)),
            sem((4, 18)),
            sem((4, 18)),
            sem((30,)),
            sem((30,)),
        ],
        compiler_params=pltpu.CompilerParams(
            collective_id=0, has_side_effects=True, vmem_limit_bytes=62 * 2**20
        ),
        name="layer",
    )(
        span_order,
        norm_gain.reshape(8, 512),
        queries,
        jnp.stack([keys, values]),
        ffn_input,
        gate_w.reshape(2, 128, 896),
        up_w.reshape(2, 128, 896),
        down_w.reshape(2, 448, 256),
    )


def solution(mesh):
    placed = (
        P("ctx", "kvh"), P("ctx", "kvh"), P("ctx", "kvh"), P(), P("ctx", "kvh"), P(),
        P("ctx", "kvh"), P("ctx", "kvh"), P("kvh", "ctx"),
    )
    return jax.shard_map(
        body,
        mesh=mesh,
        in_specs=placed,
        out_specs=(P("ctx", "kvh"), P("kvh", "ctx"), P("ctx", "kvh")),
        check_vma=False,
    )
```

time: 497 us -> 192 us (0.39)
  the two profiles are of different devices: /device:TPU:0 before, /device:TPU:1 now
where the time goes in v1:
time: 192 us; the launch traced here: 191 us
  Pallas kernels  184 us (96%)
  local copies, waits for them, and re-layouts  4.65 us (2%)
    pallas_call x1, Pallas kernels, body(): pl.pallas_call(kernel, out_shape=(jax.ShapeDtypeStruct((512, 512), BF), j...  184 us

profile of v1, /device:TPU:1, one launch (start us, length us, event | category | flops | bytes accessed | tf_op | source)
XLA Modules:
  0.0 191.5 jit_solution(13158390693346934178)
XLA Ops:
  0.6 1.3 reshape.18.gain_ref
  2.0 1.7 pad_maximum_fusion.kv_in
  3.7 184.5 %layer.1 = (bf16[512,512]{1,0:T(8,128)(2,1)}, f32[4,512]{1,0:T(4,128)}, bf16[512,512]{1,0:T(8,128)(2,1)}) custom-call(s32[16]{0:T(128)} %span_ref.1, f32[8,512]{1,0:T(8,128)} %reshape.18.gain_ref, bf16[512,512]{1,0:T(8,128)(2,1)} %q_in.1, bf16[2,512,128]{2,1,0:T(8,128)(2,1)} %pad_maximum_fusion.kv_in, bf16[512,512]{1,0:T(8,128)(2,1)} %f_in.1, ...), custom_call_target="tpu_custom_call" | custom-call | tf_op jit(solution)/shard_map/layer/pallas_call | solution.py:485
  188.1 0.0 copy-start.1
  188.1 0.0 copy-start
  188.2 1.9 %copy.15 = bf16[512,512]{1,0:T(8,128)(2,1)} copy(bf16[512,512]{1,0:T(8,128)(2,1)} %get-tuple-element.6) | data formatting | bytes 1048576
  190.1 0.0 copy-done.1
  190.1 0.6 copy.16
  190.7 0.0 copy-done
  190.7 0.8 copy.17
Async XLA Ops:
  188.1 1.9 %copy-start.1 = (f32[4,512]{1,0:T(4,128)S(1)}, f32[4,512]{1,0:T(4,128)}, u32[]{:S(2)}) copy-start(f32[4,512]{1,0:T(4,128)} %get-tuple-element.7) | copy-start | bytes 24580
  188.1 2.5 %copy-start = (bf16[512,512]{1,0:T(8,128)(2,1)S(1)}, bf16[512,512]{1,0:T(8,128)(2,1)}, u32[]{:S(2)}) copy-start(bf16[512,512]{1,0:T(8,128)(2,1)} %get-tuple-element.8) | copy-start | bytes 1572868

commit v2 on v1

v2 whole, which is shorter than its diff:
```python
import functools
import math

import jax
import jax.numpy as jnp
from jax import lax
from jax.experimental import pallas as pl
from jax.experimental.pallas import tpu as pltpu
from jax.sharding import PartitionSpec as P

MESH = pl.DeviceIdType.MESH
HD = 128
TOK = 512
BF = jnp.bfloat16
F32 = jnp.float32
KV, GATE, UP, DOWN = range(4)
LOG2E = math.log2(math.e)
SCALE2 = LOG2E / math.sqrt(HD)

ORDER = (
    "st", "K0", "F0a", "G0", "U0", "K1", "Fs", "Q", "K2", "G1", "G2", "F1a", "F2a", "K3", "U4",
    "U1", "U2", "Kr0", "A00", "G3", "K4", "A01", "A02", "A03", "U8", "Gr0", "F0b", "G4", "Ur0",
    "U5", "K5", "K6", "U6", "Kr1", "A10", "U3", "U9", "F1b", "F2b", "Kr2", "A11", "A12", "U10",
    "A13", "Ur1", "G5", "G6", "A20", "U7", "A21", "Ur2", "F3", "D0", "K7", "N", "Gr1", "PG0", "Gr2",
    "Kr3", "PG1", "U11", "PG2", "D2", "PU0", "G7", "D1", "PU1", "Ur3", "PU2", "PU3", "Gr3", "D3",
    "PG3", "ACT", "A22", "Dr0", "W02", "W00", "W01", "W03", "A23", "D4", "A30", "X00", "X01", "A31",
    "D5", "D6", "A32", "A33", "C0", "AF", "Dr1", "W12", "W10", "W11", "Dr2", "W22", "W20", "W21",
    "E0", "W13", "W23", "X10", "X11", "D7", "X20", "Dr3", "X21", "W32", "W30", "W31", "W33", "C1",
    "C2", "E1", "X30", "X31", "E2", "C3", "E3",
)


def kernel(
    span_ref, gain_ref, q_in, kv_in, f_in, g_in, u_in, d_in,
    att_out, log_out, ffn_out,
    kv_b, g_b, u_b, d_b,
    q_b, f_b, n_b, m_b, acc_b, o_b, orx_b, lg_b, lrx_b,
    ga_b, ua_b, hid_b, ps_b, po_b, fr_b, rs_b, r_b, rx_b, fs_b, fo_b,
    loc_sem, send_sem, recv_sem, xs_sem, xr_sem,
):
    ctx = lax.axis_index("ctx")
    kvh = lax.axis_index("kvh")
    x, c = kvh // 2, kvh % 2
    y, z = ctx // 4, ctx % 4
    h = y // 2
    same = c * h + (1 - c) * (1 - h)
    is_same = c == h
    not_same = c != h
    yp = y + 1 - 2 * (y % 2)
    yo = 3 - y
    yq = (y + 2) % 4
    yt = same * y + (1 - same) * yo

    def dev(xx, yy, zz, cc):
        return {"ctx": yy * 4 + zz, "kvh": xx * 2 + cc}

    zr, zl, zf = (z + 1) % 4, (z + 3) % 4, (z + 2) % 4
    xr, xl = (x + 1) % 4, (x + 3) % 4
    SIB = dev(x, y, z, 1 - c)
    PART = dev(x, yp, z, c)
    OPP = dev(x, yo, z, c)
    OPPD = dev(x, yo, z, 1 - c)
    ZR, ZL = dev(x, y, zr, c), dev(x, y, zl, c)
    XR, XL = dev(xr, y, z, c), dev(xl, y, z, c)

    barrier = pltpu.get_barrier_semaphore()
    for t in (SIB, PART, OPP, OPPD, ZR, ZL, XR, XL):
        pl.semaphore_signal(barrier, inc=1, device_id=t, device_id_type=MESH)
    pl.semaphore_wait(barrier, 8)

    def remote(src, dst, ss, rs, target):
        return pltpu.make_async_remote_copy(
            src_ref=src, dst_ref=dst, send_sem=ss, recv_sem=rs,
            device_id=target, device_id_type=MESH,
        )

    bufs = (kv_b, g_b, u_b, d_b)
    ins = (kv_in, g_in, u_in, d_in)
    groups = (z, zl, zr, zf)
    own = 4 * z + y
    extra = (16, 16, 16 + z, 16)
    yb = (y, yp, yo, yq)
    P0 = 2 * h
    P1 = 2 - 2 * h
    sent = {}

    def copy_of(a, idx):
        def cp(s, d, target, count=1):
            if count == 1:
                src, dst = bufs[a].at[s, c], bufs[a].at[d, c]
            else:
                src = bufs[a].at[pl.ds(s, count), c]
                dst = bufs[a].at[pl.ds(d, count), c]
            return remote(src, dst, send_sem.at[a, idx], recv_sem.at[a, idx], target)

        if idx == 0:
            slot = same * own + (1 - same) * extra[a]
            return remote(
                ins[a].at[1 - c], bufs[a].at[slot, 1 - c],
                send_sem.at[a, 0], recv_sem.at[a, 0], SIB,
            )
        if 14 <= idx < 18:
            s = 4 * groups[idx - 14]
            return cp(s, s, SIB, 4)
        if a == UP:
            if idx in (4, 6):
                return cp(own, own, ZR if idx == 4 else ZL)
            if idx in (5, 7):
                return cp(16 + z, 16 + z, ZR if idx == 5 else ZL)
            if idx == 8:
                return cp(4 * zl + y, 4 * zl + y, ZR)
            if idx == 9:
                return cp(16 + zr, 16 + zr, ZL)
            zs = groups[idx % 4]
            if 20 <= idx < 24:
                return cp(4 * zs + y, 4 * zs + y, PART)
            if 24 <= idx < 28:
                return cp(16 + zs, 4 * zs + y, OPP)
            return cp(4 * zs + yo, 4 * zs + yo, PART)
        if idx == 1:
            return cp(own, own, PART)
        if idx == 2:
            return cp(16, own, OPP)
        if idx == 3:
            return cp(4 * z + yo, 4 * z + yo, PART)
        if 4 <= idx < 12:
            s = 4 * z + yb[idx % 4]
            return cp(s, s, ZR if idx < 8 else ZL)
        if idx == 12:
            return cp(4 * zl + P0, 4 * zl + P0, ZR, 2)
        return cp(4 * zr + P1, 4 * zr + P1, ZL, 2)

    def local_of(a):
        slot = same * own + (1 - same) * extra[a]
        return pltpu.make_async_copy(ins[a].at[c], bufs[a].at[slot, c], loc_sem.at[a])

    def go(a, *idxs):
        for idx in idxs:
            copy_of(a, idx).start()
            sent[a, idx] = True

    def got(a, *idxs):
        for idx in idxs:
            copy_of(a, idx).wait_recv()

    def ev_z(a, n):
        if n == 0:
            local_of(a).wait()
            got(a, 0)
            go(a, 1, 2, 4, 8)
        elif n == 1:
            got(a, 1)
            go(a, 5, 9)
        elif n == 2:
            got(a, 2)
            go(a, 3, 6, 10)
        elif n == 3:
            got(a, 3)
            go(a, 7, 11, 14)
        elif n == 4:
            got(a, 4, 5)
            go(a, 12)
        elif n == 5:
            got(a, 10, 11)
            go(a, 13)
        elif n == 6:
            got(a, 6, 7)
            go(a, 15)
            got(a, 8, 9)
            go(a, 16)
        elif n == 7:
            got(a, 12, 13)
            go(a, 17)

    def ev_y(a, n):
        if n == 0:
            local_of(a).wait()
            got(a, 0)
            go(a, 4, 7, 5, 6, 20, 24)
        elif n == 1:
            got(a, 4, 5)
            go(a, 8, 21, 25)
        elif n == 2:
            got(a, 6, 7)
            go(a, 9, 22, 26)
        elif n == 3:
            got(a, 8, 9)
            go(a, 23, 27)
        elif n < 8:
            got(a, 20 + n)
            go(a, 24 + n)
        else:
            got(a, 12 + n, 20 + n)
            go(a, 6 + n)

    k0 = 2 * x + c
    two = pl.ds(2 * x, 2)

    def xc(i, j=0):
        def cp(src, dst, target):
            return remote(src, dst, xs_sem.at[i], xr_sem.at[i], target)

        if i == 0:
            return cp(f_in, f_b.at[k0], SIB)
        if i in (1, 2):
            return remote(
                f_in, f_b.at[k0], xs_sem.at[1], xr_sem.at[1 + c], OPP if i == 1 else OPPD
            )
        if i == 3:
            return cp(q_in, q_b, OPPD)
        if i in (4, 5):
            return cp(f_b.at[two], f_b.at[two], XR if i == 4 else XL)
        if i == 6:
            return cp(f_b.at[2 * xl], f_b.at[2 * xl], XR)
        if i == 7:
            return cp(f_b.at[2 * xr + 1], f_b.at[2 * xr + 1], XL)
        if i == 8:
            return cp(o_b, orx_b, OPPD)
        if i == 9:
            return cp(lg_b, lrx_b, OPPD)
        if i < 14:
            return cp(r_b.at[i - 10], rx_b.at[i - 10], OPP)
        if i < 18:
            n = i - 14
            sub = groups[n] % 2
            return remote(fs_b.at[n], fo_b.at[sub], xs_sem.at[i], xr_sem.at[14 + sub], SIB)
        g, n = (i - 18) // 6, (i - 18) % 6
        lo, hi = pl.ds(0, 256), pl.ds(256, 256)
        if n == 0:
            return cp(ps_b.at[g, 2, lo], fr_b.at[g, 0], XR)
        if n == 1:
            return cp(ps_b.at[g, 2, hi], fr_b.at[g, 1], XL)
        if n == 2:
            return cp(ps_b.at[g, 0, hi], rs_b.at[g, 0, hi], XR)
        if n == 3:
            return cp(ps_b.at[g, 1, lo], rs_b.at[g, 1, lo], XL)
        if n == 4:
            return cp(ps_b.at[g, 0, lo], rs_b.at[g, 0, lo], XR)
        return cp(ps_b.at[g, 1, hi], rs_b.at[g, 1, hi], XL)

    f_loc = pltpu.make_async_copy(f_in, f_b.at[k0], loc_sem.at[4])
    q_loc = pltpu.make_async_copy(q_in, q_b, loc_sem.at[5])

    def start():
        @pl.when(is_same)
        def _():
            f_loc.start()
            q_loc.start()

        @pl.when(not_same)
        def _():
            xc(0).start()
            xc(3).start()

        for a in (KV, GATE, UP, DOWN):
            local_of(a).start()
            go(a, 0)

    def feat(nm):
        if nm == "Fs":
            pl.when(is_same)(lambda: xc(1).start())
            pl.when(not_same)(lambda: xc(2).start())
            return
        n = nm[1]
        if n == "3":
            xc(6).wait_recv()
            xc(7).wait_recv()
            return

        @pl.when(is_same if nm[2] == "a" else not_same)
        def _():
            if nm == "F0a":
                f_loc.wait()
                xc(0).wait_recv()
            elif nm == "F0b":
                for j in range(2):
                    remote(f_in, f_b.at[0], xs_sem.at[1], xr_sem.at[1 + j], OPP).wait_recv()
            if n == "0":
                xc(4).start()
                xc(5).start()
            elif n == "1":
                xc(4).wait_recv()
                xc(6).start()
            else:
                xc(5).wait_recv()
                xc(7).start()

    def q_wait():
        pl.when(is_same)(lambda: q_loc.wait())
        pl.when(not_same)(lambda: xc(3).wait())

    my_span = span_ref[yt * 4 + z]

    def attend(slot, src, first):
        hide = jnp.where(span_ref[src] < my_span, 0.0, 1e30).astype(F32)
        k = kv_b[slot, 0]
        va = jnp.concatenate([kv_b[slot, 1], jnp.ones((TOK, HD), BF)], axis=1)
        step = 128
        for g in range(4):
            for t in range(TOK // step):
                rows = slice(t * step, t * step + step)
                q = q_b[rows, g * HD : g * HD + HD]
                s = lax.dot_general(q, k, (((1,), (1,)), ((), ())), preferred_element_type=F32)
                if first:
                    ri = lax.broadcasted_iota(jnp.int32, (step, TOK), 0) + t * step
                    ci = lax.broadcasted_iota(jnp.int32, (step, TOK), 1)
                    s = jnp.where(ci <= ri, s, -1e30)
                    m_new = jnp.broadcast_to(jnp.max(s, axis=1, keepdims=True), (step, HD)) * SCALE2
                    p = jnp.exp2(s * SCALE2 - jnp.concatenate([m_new] * 4, axis=1))
                    acc_b[g, rows] = jnp.dot(p.astype(BF), va, preferred_element_type=F32)
                else:
                    m_old = m_b[g, rows]
                    top = jnp.max(s, axis=1, keepdims=True) * SCALE2 - hide
                    m_new = jnp.maximum(m_old, top)
                    alpha = jnp.exp2(m_old - m_new)
                    sub = m_new + hide
                    p = jnp.exp2(s * SCALE2 - jnp.concatenate([sub] * 4, axis=1))
                    pv = jnp.dot(p.astype(BF), va, preferred_element_type=F32)
                    acc_b[g, rows] = acc_b[g, rows] * jnp.concatenate([alpha] * 2, axis=1) + pv
                m_b[g, rows] = m_new

    def finish():
        for g in range(4):
            col = g * HD
            total = acc_b[g, :, HD:]
            o_b[:, col : col + HD] = (acc_b[g, :, :HD] / total).astype(BF)
            logs = m_b[g] * (1.0 / LOG2E) + jnp.log(total)
            lg_b[g] = jnp.transpose(logs)[:8]

        @pl.when(is_same)
        def _():
            att_out[...] = o_b[...]
            for g in range(4):
                log_out[pl.ds(g, 1)] = lg_b[g, :1]

        @pl.when(not_same)
        def _():
            xc(8).start()
            xc(9).start()

    def norm():
        def rows_of(i, _):
            rows = pl.ds(i * 64, 64)
            part = jnp.zeros((64, TOK), F32)
            for k in range(8):
                v = f_b[k, rows].astype(F32)
                part = part + v * v
            r = lax.rsqrt(jnp.sum(part, axis=1, keepdims=True) * (1.0 / 4096) + 1e-05)
            for k in range(8):
                n_b[k, rows] = (f_b[k, rows].astype(F32) * r * gain_ref[pl.ds(k, 1)]).astype(BF)
            return 0

        lax.fori_loop(0, 8, rows_of, 0)

    def project(a, i):
        zs = groups[i]
        out = ga_b if a == GATE else ua_b
        off = pl.multiple_of((zs % 2) * 256, 256)

        def rows_of(t, _):
            rows = pl.ds(t * 256, 256)
            lhs = jnp.concatenate(
                [n_b[2 * ys + zs // 2, rows, pl.ds(off, 256)] for ys in range(4)], axis=1
            )
            w = bufs[a][pl.ds(4 * zs, 4)].reshape(1024, 896)
            res = jnp.dot(lhs, w, preferred_element_type=F32)
            if i == 0:
                out[rows] = res
            else:
                out[rows] = out[rows] + res
            return 0

        lax.fori_loop(0, 2, rows_of, 0)

    def act():
        def rows_of(i, _):
            rows = pl.ds(i * 64, 64)
            g = ga_b[rows]
            hid_b[rows] = (g / (1.0 + jnp.exp(-g)) * ua_b[rows]).astype(BF)
            return 0

        lax.fori_loop(0, 8, rows_of, 0)

    def x_go(i, *ns):
        for n in ns:
            xc(18 + 6 * i + n).start()
            sent[18 + 6 * i + n] = True

    def x_got(i, *ns):
        for n in ns:
            xc(18 + 6 * i + n).wait_recv()

    def down(i, n):
        xd = (xr, xl, (x + 2) % 4, x)[n]
        w = d_b[4 * groups[i] + xd].reshape(896, 256)
        res = jnp.dot(hid_b[...], w, preferred_element_type=F32)
        if n == 3:
            po_b[i] = res
            return
        ps_b[i, n] = res.astype(BF)
        if n == 2:
            x_go(i, 0, 1)
        else:
            x_go(i, 2 + n)

    def forward(i, n):
        x_got(i, n)
        rows = pl.ds(256 * n, 256)
        ps_b[i, n, rows] = (ps_b[i, n, rows].astype(F32) + fr_b[i, n].astype(F32)).astype(BF)
        x_go(i, 4 + n)

    def combine(i):
        x_got(i, 2, 3, 4, 5)
        po_b[i] = po_b[i] + rs_b[i, 0].astype(F32) + rs_b[i, 1].astype(F32)

        @pl.when(not_same)
        def _():
            r_b[i] = po_b[i].astype(BF)
            xc(10 + i).start()

    def close(i):
        zs = groups[i]
        off = pl.multiple_of((zs % 2) * 256, 256)

        @pl.when(is_same)
        def _():
            xc(10 + i).wait_recv()
            res = (po_b[i] + rx_b[i].astype(F32)).astype(BF)

            @pl.when(zs // 2 == c)
            def _():
                ffn_out[:, pl.ds(off, 256)] = res

            @pl.when(zs // 2 != c)
            def _():
                fs_b[i] = res
                xc(14 + i).start()

    def run(nm):
        if nm == "st":
            start()
        elif nm[0] == "F":
            feat(nm)
        elif nm == "Q":
            q_wait()
        elif nm == "AF":
            finish()
        elif nm == "N":
            norm()
        elif nm == "ACT":
            act()
        elif nm[0] == "P":
            project("KGUD".index(nm[1]), int(nm[2]))
        elif nm[0] == "W":
            down(int(nm[1]), int(nm[2]))
        elif nm[0] == "X":
            forward(int(nm[1]), int(nm[2]))
        elif nm[0] == "C":
            combine(int(nm[1]))
        elif nm[0] == "E":
            close(int(nm[1]))
        else:
            a = "KGUD".index(nm[0])
            if nm[1] == "r":
                got(a, 14 + int(nm[2]))
            elif a == UP:
                ev_y(a, int(nm[1:]))
            else:
                ev_z(a, int(nm[1:]))

    parts = [[]]
    for nm in ORDER:
        if nm[0] == "A" and nm[1:].isdigit():
            parts.append([])
        else:
            parts[-1].append(nm)
    for nm in parts[0]:
        run(nm)
    attend(4 * z + yt, yt * 4 + z, True)
    for nm in parts[1]:
        run(nm)

    def block(n, _):
        i, j = n // 4, n % 4
        delta = (i // 2) * (i - 1) + (1 - i // 2) * (3 * i)
        zs = (z + delta) % 4
        ys = (yt + j) % 4
        attend(4 * zs + ys, ys * 4 + zs, False)
        for m in range(1, 15):
            if parts[m + 1]:
                @pl.when(n == m)
                def _():
                    for nm in parts[m + 1]:
                        run(nm)
        return 0

    lax.fori_loop(1, 16, block, 0)
    for nm in parts[16]:
        run(nm)

    @pl.when(is_same)
    def _():
        xc(1).wait_send()
        for i in range(4):
            pl.when(groups[i] // 2 != c)(lambda: xc(14 + i).wait_send())

    @pl.when(not_same)
    def _():
        xc(0).wait_send()
        xc(2).wait_send()
        xc(8).wait()
        xc(9).wait()
        att_out[...] = orx_b[...]
        for g in range(4):
            log_out[pl.ds(g, 1)] = lrx_b[g, :1]
        for i in range(4):
            xc(10 + i).wait_send()
        for s in range(2):
            remote(fs_b.at[0], fo_b.at[s], xs_sem.at[14], xr_sem.at[14 + s], SIB).wait_recv()
            ffn_out[:, s * 256 : (s + 1) * 256] = fo_b[s]

    for i in (4, 5, 6, 7):
        xc(i).wait_send()
    for it in sent:
        if isinstance(it, tuple):
            copy_of(*it).wait_send()
        else:
            xc(it).wait_send()


def body(queries, keys, values, span_order, ffn_input, norm_gain, gate_w, up_w, down_w):
    anyspace = pl.BlockSpec(memory_space=pl.ANY)
    vmem = pl.BlockSpec(memory_space=pltpu.VMEM)
    smem = pl.BlockSpec(memory_space=pltpu.SMEM)
    sem = pltpu.SemaphoreType.DMA
    return pl.pallas_call(
        kernel,
        out_shape=(
            jax.ShapeDtypeStruct((512, 512), BF),
            jax.ShapeDtypeStruct((4, 512), F32),
            jax.ShapeDtypeStruct((512, 512), BF),
        ),
        in_specs=[smem, vmem] + [anyspace] * 6,
        out_specs=(vmem, vmem, vmem),
        scratch_shapes=[
            pltpu.VMEM((17, 2, 512, 128), BF),
            pltpu.VMEM((17, 2, 128, 896), BF),
            pltpu.VMEM((20, 2, 128, 896), BF),
            pltpu.VMEM((17, 2, 448, 256), BF),
            pltpu.VMEM((512, 512), BF),
            pltpu.VMEM((8, 512, 512), BF),
            pltpu.VMEM((8, 512, 512), BF),
            pltpu.VMEM((4, 512, 128), F32),
            pltpu.VMEM((4, 512, 256), F32),
            pltpu.VMEM((512, 512), BF),
            pltpu.VMEM((512, 512), BF),
            pltpu.VMEM((4, 8, 512), F32),
            pltpu.VMEM((4, 8, 512), F32),
            pltpu.VMEM((512, 896), F32),
            pltpu.VMEM((512, 896), F32),
            pltpu.VMEM((512, 896), BF),
            pltpu.VMEM((4, 3, 512, 256), BF),
            pltpu.VMEM((4, 512, 256), F32),
            pltpu.VMEM((4, 2, 256, 256), BF),
            pltpu.VMEM((4, 2, 512, 256), BF),
            pltpu.VMEM((4, 512, 256), BF),
            pltpu.VMEM((4, 512, 256), BF),
            pltpu.VMEM((4, 512, 256), BF),
            pltpu.VMEM((2, 512, 256), BF),
            sem((6,)),
            sem((4, 32)),
            sem((4, 32)),
            sem((42,)),
            sem((42,)),
        ],
        compiler_params=pltpu.CompilerParams(
            collective_id=0, has_side_effects=True, vmem_limit_bytes=63 * 2**20
        ),
        name="layer",
    )(
        span_order,
        norm_gain.reshape(8, 512),
        queries,
        jnp.stack([keys, values]),
        ffn_input,
        gate_w.reshape(2, 128, 896),
        up_w.reshape(2, 128, 896),
        down_w.reshape(2, 448, 256),
    )


def solution(mesh):
    placed = (
        P("ctx", "kvh"), P("ctx", "kvh"), P("ctx", "kvh"), P(), P("ctx", "kvh"), P(),
        P("ctx", "kvh"), P("ctx", "kvh"), P("kvh", "ctx"),
    )
    return jax.shard_map(
        body,
        mesh=mesh,
        in_specs=placed,
        out_specs=(P("ctx", "kvh"), P("kvh", "ctx"), P("ctx", "kvh")),
        check_vma=False,
    )
```

time: 192 us -> 144 us (0.75)
  Pallas kernels: 184 us -> 136 us
    pallas_call x1, Pallas kernels: 184 us -> 136 us  [body(): pl.pallas_call(kernel, out_shape=(jax.ShapeDtypeStruct((512, 512), BF), j...]
where the time goes in v2:
time: 144 us; the launch traced here: 143 us
  Pallas kernels  136 us (94%)
  local copies, waits for them, and re-layouts  4.65 us (3%)
  other arithmetic  1.69 us (1%)
    pallas_call x1, Pallas kernels, body(): pl.pallas_call(kernel, out_shape=(jax.ShapeDtypeStruct((512, 512), BF), j...  136 us
    unnamed x7, local copies, waits for them, and re-layouts  3.33 us

profile of v2, /device:TPU:1, one launch (start us, length us, event | category | flops | bytes accessed | tf_op | source)
XLA Modules:
  0.0 143.4 jit_solution(4380469971480365829)
XLA Ops:
  0.6 1.3 reshape.18.gain_ref
  2.0 1.7 %pad_maximum_fusion.kv_in = bf16[2,512,128]{2,1,0:T(8,128)(2,1)} fusion(bf16[1,512,128]{2,1,0:T(8,128)(2,1)} %bitcast.8, bf16[1,512,128]{2,1,0:T(8,128)(2,1)} %bitcast.9), kind=kLoop, calls=%fused_computation | loop fusion | flops 131072 | bytes 524288 | tf_op jit(solution)/shard_map/stack | solution.py:584
  3.7 136.4 %layer.1 = (bf16[512,512]{1,0:T(8,128)(2,1)}, f32[4,512]{1,0:T(4,128)}, bf16[512,512]{1,0:T(8,128)(2,1)}) custom-call(s32[16]{0:T(128)} %span_ref.1, f32[8,512]{1,0:T(8,128)} %reshape.18.gain_ref, bf16[512,512]{1,0:T(8,128)(2,1)} %q_in.1, bf16[2,512,128]{2,1,0:T(8,128)(2,1)} %pad_maximum_fusion.kv_in, bf16[512,512]{1,0:T(8,128)(2,1)} %f_in.1, ...), custom_call_target="tpu_custom_call" | custom-call | tf_op jit(solution)/shard_map/layer/pallas_call | solution.py:536
  140.0 0.0 copy-start.1
  140.0 0.0 copy-start
  140.0 1.9 %copy.15 = bf16[512,512]{1,0:T(8,128)(2,1)} copy(bf16[512,512]{1,0:T(8,128)(2,1)} %get-tuple-element.6) | data formatting | bytes 1048576
  142.0 0.0 copy-done.1
  142.0 0.6 copy.16
  142.6 0.0 copy-done
  142.6 0.8 copy.17
Async XLA Ops:
  140.0 1.9 %copy-start.1 = (f32[4,512]{1,0:T(4,128)S(1)}, f32[4,512]{1,0:T(4,128)}, u32[]{:S(2)}) copy-start(f32[4,512]{1,0:T(4,128)} %get-tuple-element.7) | copy-start | bytes 24580
  140.0 2.5 %copy-start = (bf16[512,512]{1,0:T(8,128)(2,1)S(1)}, bf16[512,512]{1,0:T(8,128)(2,1)}, u32[]{:S(2)}) copy-start(bf16[512,512]{1,0:T(8,128)(2,1)} %get-tuple-element.8) | copy-start | bytes 1572868

commit v3 on v2

--- a/solution.py
+++ b/solution.py
@@ -18,24 +18,24 @@
 SCALE2 = LOG2E / math.sqrt(HD)
 
 ORDER = (
-    "st", "K0", "F0a", "G0", "U0", "K1", "Fs", "Q", "K2", "G1", "G2", "F1a", "F2a", "K3", "U4",
-    "U1", "U2", "Kr0", "A00", "G3", "K4", "A01", "A02", "A03", "U8", "Gr0", "F0b", "G4", "Ur0",
-    "U5", "K5", "K6", "U6", "Kr1", "A10", "U3", "U9", "F1b", "F2b", "Kr2", "A11", "A12", "U10",
-    "A13", "Ur1", "G5", "G6", "A20", "U7", "A21", "Ur2", "F3", "D0", "K7", "N", "Gr1", "PG0", "Gr2",
-    "Kr3", "PG1", "U11", "PG2", "D2", "PU0", "G7", "D1", "PU1", "Ur3", "PU2", "PU3", "Gr3", "D3",
-    "PG3", "ACT", "A22", "Dr0", "W02", "W00", "W01", "W03", "A23", "D4", "A30", "X00", "X01", "A31",
-    "D5", "D6", "A32", "A33", "C0", "AF", "Dr1", "W12", "W10", "W11", "Dr2", "W22", "W20", "W21",
-    "E0", "W13", "W23", "X10", "X11", "D7", "X20", "Dr3", "X21", "W32", "W30", "W31", "W33", "C1",
-    "C2", "E1", "X30", "X31", "E2", "C3", "E3",
+    "st", "K0", "F0a", "G0", "U0", "K4", "G1", "G2", "Fs", "F1a", "U4", "K8", "Kr0", "G3", "U1",
+    "U2", "Q", "Gr0", "U8", "G4", "F2a", "F0b", "U5", "G5", "G6", "U6", "Gr1", "U3", "U9", "Gr2",
+    "D0", "F2b", "F1b", "U10", "Ur1", "A00", "A01", "U7", "A02", "Ur2", "G7", "A03", "D2", "F3",
+    "Ur0", "K1", "N", "D1", "Gr3", "PU0", "PU2", "K5", "K2", "PU1", "U11", "PG0", "PG3", "PG1",
+    "K6", "D3", "Ur3", "PU3", "PG2", "K3", "D4", "ACT", "Dr0", "W02", "W01", "K9", "W03", "W00",
+    "D5", "D6", "K7", "Kr1", "A10", "X01", "X00", "K10", "A11", "Dr1", "W10", "W11", "W12", "A12",
+    "Dr2", "W21", "W23", "Kr2", "C0", "K11", "W20", "W22", "A13", "D7", "A20", "X10", "E0", "X11",
+    "Kr3", "A21", "A22", "Dr3", "W33", "W32", "W30", "A23", "X21", "X20", "A30", "W13", "C1", "A31",
+    "X30", "W31", "X31", "A32", "A33", "E1", "AF", "C2", "C3", "E2", "E3",
 )
 
 
 def kernel(
-    span_ref, gain_ref, q_in, kv_in, f_in, g_in, u_in, d_in,
+    span_ref, gain_ref, q_in, k_in, v_in, f_in, g_in, u_in, d_in,
     att_out, log_out, ffn_out,
     kv_b, g_b, u_b, d_b,
     q_b, f_b, n_b, m_b, acc_b, o_b, orx_b, lg_b, lrx_b,
-    ga_b, ua_b, hid_b, ps_b, po_b, fr_b, rs_b, r_b, rx_b, fs_b, fo_b,
+    ga_b, ua_b, hid_b, ps_b, po_b, fr_b, rs_b, r_b, rx_b, fo_b,
     loc_sem, send_sem, recv_sem, xs_sem, xr_sem,
 ):
     ctx = lax.axis_index("ctx")
@@ -75,16 +75,16 @@
         )
 
     bufs = (kv_b, g_b, u_b, d_b)
-    ins = (kv_in, g_in, u_in, d_in)
+    ins = (None, g_in, u_in, d_in)
     groups = (z, zl, zr, zf)
     own = 4 * z + y
-    extra = (16, 16, 16 + z, 16)
+    extra = (16 + z, 16, 16 + z, 16)
     yb = (y, yp, yo, yq)
     P0 = 2 * h
     P1 = 2 - 2 * h
     sent = {}
 
-    def copy_of(a, idx):
+    def copy_of(a, idx, half=0):
         def cp(s, d, target, count=1):
             if count == 1:
                 src, dst = bufs[a].at[s, c], bufs[a].at[d, c]
@@ -95,14 +95,17 @@
 
         if idx == 0:
             slot = same * own + (1 - same) * extra[a]
+            src = (v_in, k_in)[half] if a == KV else ins[a].at[1 - c]
             return remote(
-                ins[a].at[1 - c], bufs[a].at[slot, 1 - c],
-                send_sem.at[a, 0], recv_sem.at[a, 0], SIB,
+                src, bufs[a].at[slot, 1 - c], send_sem.at[a, 0], recv_sem.at[a, 0], SIB
             )
+        if idx in (17, 18) and a not in (KV, UP):
+            s = 4 * zf + (P0 if idx == 17 else P1)
+            return cp(s, s, SIB, 2)
         if 14 <= idx < 18:
             s = 4 * groups[idx - 14]
             return cp(s, s, SIB, 4)
-        if a == UP:
+        if a in (KV, UP):
             if idx in (4, 6):
                 return cp(own, own, ZR if idx == 4 else ZL)
             if idx in (5, 7):
@@ -130,9 +133,10 @@
             return cp(4 * zl + P0, 4 * zl + P0, ZR, 2)
         return cp(4 * zr + P1, 4 * zr + P1, ZL, 2)
 
-    def local_of(a):
+    def local_of(a, half=0):
         slot = same * own + (1 - same) * extra[a]
-        return pltpu.make_async_copy(ins[a].at[c], bufs[a].at[slot, c], loc_sem.at[a])
+        src = (k_in, v_in)[half] if a == KV else ins[a].at[c]
+        return pltpu.make_async_copy(src, bufs[a].at[slot, c], loc_sem.at[a])
 
     def go(a, *idxs):
         for idx in idxs:
@@ -169,8 +173,10 @@
             got(a, 8, 9)
             go(a, 16)
         elif n == 7:
-            got(a, 12, 13)
+            got(a, 12)
             go(a, 17)
+            got(a, 13)
+            go(a, 18)
 
     def ev_y(a, n):
         if n == 0:
@@ -196,7 +202,10 @@
     k0 = 2 * x + c
     two = pl.ds(2 * x, 2)
 
-    def xc(i, j=0):
+    def out_copy(g):
+        return remote(o_b.at[g], orx_b.at[g], xs_sem.at[42 + g], xr_sem.at[42 + g], OPPD)
+
+    def xc(i):
         def cp(src, dst, target):
             return remote(src, dst, xs_sem.at[i], xr_sem.at[i], target)
 
@@ -214,16 +223,13 @@
             return cp(f_b.at[2 * xl], f_b.at[2 * xl], XR)
         if i == 7:
             return cp(f_b.at[2 * xr + 1], f_b.at[2 * xr + 1], XL)
-        if i == 8:
-            return cp(o_b, orx_b, OPPD)
         if i == 9:
             return cp(lg_b, lrx_b, OPPD)
         if i < 14:
-            return cp(r_b.at[i - 10], rx_b.at[i - 10], OPP)
+            n = i - 10
+            return cp(r_b.at[n], rx_b.at[n], {"ctx": yo * 4 + z, "kvh": 2 * x + groups[n] // 2})
         if i < 18:
-            n = i - 14
-            sub = groups[n] % 2
-            return remote(fs_b.at[n], fo_b.at[sub], xs_sem.at[i], xr_sem.at[14 + sub], SIB)
+            return cp(r_b.at[i - 14], fo_b.at[i - 14], SIB)
         g, n = (i - 18) // 6, (i - 18) % 6
         lo, hi = pl.ds(0, 256), pl.ds(256, 256)
         if n == 0:
@@ -252,7 +258,14 @@
             xc(0).start()
             xc(3).start()
 
-        for a in (KV, GATE, UP, DOWN):
+        for half in range(2):
+            @pl.when(c == half)
+            def _():
+                local_of(KV, half).start()
+                copy_of(KV, 0, half).start()
+
+        sent[KV, 0] = True
+        for a in (GATE, UP, DOWN):
             local_of(a).start()
             go(a, 0)
 
@@ -291,54 +304,70 @@
 
     my_span = span_ref[yt * 4 + z]
 
-    def attend(slot, src, first):
+    step = 128
+
+    def tile(g, t, q, k, va, hide, first):
+        rows = slice(t * step, t * step + step)
+        s = lax.dot_general(q, k, (((1,), (1,)), ((), ())), preferred_element_type=F32)
+        if first:
+            ri = lax.broadcasted_iota(jnp.int32, (step, TOK), 0) + t * step
+            ci = lax.broadcasted_iota(jnp.int32, (step, TOK), 1)
+            s = jnp.where(ci <= ri, s, -1e30)
+            m_new = jnp.broadcast_to(jnp.max(s, axis=1, keepdims=True), (step, HD)) * SCALE2
+            p = jnp.exp2(s * SCALE2 - jnp.concatenate([m_new] * 4, axis=1))
+            acc_b[g, rows] = jnp.dot(p.astype(BF), va, preferred_element_type=F32)
+        else:
+            m_old = m_b[g, rows]
+            top = jnp.max(s, axis=1, keepdims=True) * SCALE2 - hide
+            m_new = jnp.maximum(m_old, top)
+            alpha = jnp.exp2(m_old - m_new)
+            sub = m_new + hide
+            p = jnp.exp2(s * SCALE2 - jnp.concatenate([sub] * 4, axis=1))
+            pv = jnp.dot(p.astype(BF), va, preferred_element_type=F32)
+            acc_b[g, rows] = acc_b[g, rows] * jnp.concatenate([alpha] * 2, axis=1) + pv
+        m_b[g, rows] = m_new
+
+    def operands(slot, src):
         hide = jnp.where(span_ref[src] < my_span, 0.0, 1e30).astype(F32)
         k = kv_b[slot, 0]
-        va = jnp.concatenate([kv_b[slot, 1], jnp.ones((TOK, HD), BF)], axis=1)
-        step = 128
+        return hide, k, jnp.concatenate([kv_b[slot, 1], jnp.ones((TOK, HD), BF)], axis=1)
+
+    def attend(slot, src, first):
+        hide, k, va = operands(slot, src)
         for g in range(4):
             for t in range(TOK // step):
-                rows = slice(t * step, t * step + step)
-                q = q_b[rows, g * HD : g * HD + HD]
-                s = lax.dot_general(q, k, (((1,), (1,)), ((), ())), preferred_element_type=F32)
-                if first:
-                    ri = lax.broadcasted_iota(jnp.int32, (step, TOK), 0) + t * step
-                    ci = lax.broadcasted_iota(jnp.int32, (step, TOK), 1)
-                    s = jnp.where(ci <= ri, s, -1e30)
-                    m_new = jnp.broadcast_to(jnp.max(s, axis=1, keepdims=True), (step, HD)) * SCALE2
-                    p = jnp.exp2(s * SCALE2 - jnp.concatenate([m_new] * 4, axis=1))
-                    acc_b[g, rows] = jnp.dot(p.astype(BF), va, preferred_element_type=F32)
-                else:
-                    m_old = m_b[g, rows]
-                    top = jnp.max(s, axis=1, keepdims=True) * SCALE2 - hide
-                    m_new = jnp.maximum(m_old, top)
-                    alpha = jnp.exp2(m_old - m_new)
-                    sub = m_new + hide
-                    p = jnp.exp2(s * SCALE2 - jnp.concatenate([sub] * 4, axis=1))
-                    pv = jnp.dot(p.astype(BF), va, preferred_element_type=F32)
-                    acc_b[g, rows] = acc_b[g, rows] * jnp.concatenate([alpha] * 2, axis=1) + pv
-                m_b[g, rows] = m_new
+                q = q_b[t * step : t * step + step, g * HD : g * HD + HD]
+                tile(g, t, q, k, va, hide, first)
+
+    def attend_head(g):
+        col = pl.ds(pl.multiple_of(g * HD, HD), HD)
+        for ys in range(4):
+            hide, k, va = operands(4 * zf + ys, 4 * ys + zf)
+            for t in range(TOK // step):
+                tile(g, t, q_b[t * step : t * step + step, col], k, va, hide, False)
+        total = acc_b[g, :, HD:]
+        o_b[g] = (acc_b[g, :, :HD] / total).astype(BF)
+        logs = m_b[g] * (1.0 / LOG2E) + jnp.log(total)
+        lg_b[g] = jnp.transpose(logs)[:8]
+
+        @pl.when(not_same)
+        def _():
+            out_copy(g).start()
 
     def finish():
-        for g in range(4):
-            col = g * HD
-            total = acc_b[g, :, HD:]
-            o_b[:, col : col + HD] = (acc_b[g, :, :HD] / total).astype(BF)
-            logs = m_b[g] * (1.0 / LOG2E) + jnp.log(total)
-            lg_b[g] = jnp.transpose(logs)[:8]
-
         @pl.when(is_same)
         def _():
-            att_out[...] = o_b[...]
             for g in range(4):
+                att_out[:, g * HD : g * HD + HD] = o_b[g]
                 log_out[pl.ds(g, 1)] = lg_b[g, :1]
 
         @pl.when(not_same)
         def _():
-            xc(8).start()
             xc(9).start()
 
     def norm():
+        gains = [gain_ref[k * TOK : (k + 1) * TOK].reshape(1, TOK) for k in range(8)]
+
         def rows_of(i, _):
             rows = pl.ds(i * 64, 64)
             part = jnp.zeros((64, TOK), F32)
@@ -347,7 +376,7 @@
                 part = part + v * v
             r = lax.rsqrt(jnp.sum(part, axis=1, keepdims=True) * (1.0 / 4096) + 1e-05)
             for k in range(8):
-                n_b[k, rows] = (f_b[k, rows].astype(F32) * r * gain_ref[pl.ds(k, 1)]).astype(BF)
+                n_b[k, rows] = (f_b[k, rows].astype(F32) * r * gains[k]).astype(BF)
             return 0
 
         lax.fori_loop(0, 8, rows_of, 0)
@@ -411,30 +440,35 @@
 
     def combine(i):
         x_got(i, 2, 3, 4, 5)
-        po_b[i] = po_b[i] + rs_b[i, 0].astype(F32) + rs_b[i, 1].astype(F32)
+        total = po_b[i] + rs_b[i, 0].astype(F32) + rs_b[i, 1].astype(F32)
+        r_b[i] = total.astype(BF)
 
         @pl.when(not_same)
         def _():
-            r_b[i] = po_b[i].astype(BF)
             xc(10 + i).start()
+
+        @pl.when(is_same & (groups[i] // 2 != c))
+        def _():
+            xc(14 + i).start()
 
     def close(i):
         zs = groups[i]
         off = pl.multiple_of((zs % 2) * 256, 256)
 
-        @pl.when(is_same)
+        @pl.when(zs // 2 == c)
         def _():
             xc(10 + i).wait_recv()
-            res = (po_b[i] + rx_b[i].astype(F32)).astype(BF)
-
-            @pl.when(zs // 2 == c)
+
+            @pl.when(is_same)
             def _():
-                ffn_out[:, pl.ds(off, 256)] = res
-
-            @pl.when(zs // 2 != c)
+                res = r_b[i].astype(F32) + rx_b[i].astype(F32)
+                ffn_out[:, pl.ds(off, 256)] = res.astype(BF)
+
+            @pl.when(not_same)
             def _():
-                fs_b[i] = res
-                xc(14 + i).start()
+                xc(14 + i).wait_recv()
+                res = fo_b[i].astype(F32) + rx_b[i].astype(F32)
+                ffn_out[:, pl.ds(off, 256)] = res.astype(BF)
 
     def run(nm):
         if nm == "st":
@@ -463,7 +497,9 @@
             a = "KGUD".index(nm[0])
             if nm[1] == "r":
                 got(a, 14 + int(nm[2]))
-            elif a == UP:
+                if nm[2] == "3" and a not in (KV, UP):
+                    got(a, 18)
+            elif a in (KV, UP):
                 ev_y(a, int(nm[1:]))
             else:
                 ev_z(a, int(nm[1:]))
@@ -486,7 +522,7 @@
         zs = (z + delta) % 4
         ys = (yt + j) % 4
         attend(4 * zs + ys, ys * 4 + zs, False)
-        for m in range(1, 15):
+        for m in range(1, 12):
             if parts[m + 1]:
                 @pl.when(n == m)
                 def _():
@@ -494,7 +530,19 @@
                         run(nm)
         return 0
 
-    lax.fori_loop(1, 16, block, 0)
+    lax.fori_loop(1, 12, block, 0)
+
+    def last(g, _):
+        attend_head(g)
+        for m in range(3):
+            if parts[13 + m]:
+                @pl.when(g == m)
+                def _():
+                    for nm in parts[13 + m]:
+                        run(nm)
+        return 0
+
+    lax.fori_loop(0, 4, last, 0)
     for nm in parts[16]:
         run(nm)
 
@@ -508,16 +556,13 @@
     def _():
         xc(0).wait_send()
         xc(2).wait_send()
-        xc(8).wait()
         xc(9).wait()
-        att_out[...] = orx_b[...]
         for g in range(4):
             log_out[pl.ds(g, 1)] = lrx_b[g, :1]
+            out_copy(g).wait()
+            att_out[:, g * HD : g * HD + HD] = orx_b[g]
         for i in range(4):
             xc(10 + i).wait_send()
-        for s in range(2):
-            remote(fs_b.at[0], fo_b.at[s], xs_sem.at[14], xr_sem.at[14 + s], SIB).wait_recv()
-            ffn_out[:, s * 256 : (s + 1) * 256] = fo_b[s]
 
     for i in (4, 5, 6, 7):
         xc(i).wait_send()
@@ -540,10 +585,10 @@
             jax.ShapeDtypeStruct((4, 512), F32),
             jax.ShapeDtypeStruct((512, 512), BF),
         ),
-        in_specs=[smem, vmem] + [anyspace] * 6,
+        in_specs=[smem, vmem] + [anyspace] * 7,
         out_specs=(vmem, vmem, vmem),
         scratch_shapes=[
-            pltpu.VMEM((17, 2, 512, 128), BF),
+            pltpu.VMEM((20, 2, 512, 128), BF),
             pltpu.VMEM((17, 2, 128, 896), BF),
             pltpu.VMEM((20, 2, 128, 896), BF),
             pltpu.VMEM((17, 2, 448, 256), BF),
@@ -552,8 +597,8 @@
             pltpu.VMEM((8, 512, 512), BF),
             pltpu.VMEM((4, 512, 128), F32),
             pltpu.VMEM((4, 512, 256), F32),
-            pltpu.VMEM((512, 512), BF),
-            pltpu.VMEM((512, 512), BF),
+            pltpu.VMEM((4, 512, 128), BF),
+            pltpu.VMEM((4, 512, 128), BF),
             pltpu.VMEM((4, 8, 512), F32),
             pltpu.VMEM((4, 8, 512), F32),
             pltpu.VMEM((512, 896), F32),
@@ -566,12 +611,11 @@
             pltpu.VMEM((4, 512, 256), BF),
             pltpu.VMEM((4, 512, 256), BF),
             pltpu.VMEM((4, 512, 256), BF),
-            pltpu.VMEM((2, 512, 256), BF),
             sem((6,)),
             sem((4, 32)),
             sem((4, 32)),
-            sem((42,)),
-            sem((42,)),
+            sem((46,)),
+            sem((46,)),
         ],
         compiler_params=pltpu.CompilerParams(
             collective_id=0, has_side_effects=True, vmem_limit_bytes=63 * 2**20
@@ -579,9 +623,10 @@
         name="layer",
     )(
         span_order,
-        norm_gain.reshape(8, 512),
+        norm_gain,
         queries,
-        jnp.stack([keys, values]),
+        keys,
+        values,
         ffn_input,
         gate_w.reshape(2, 128, 896),
         up_w.reshape(2, 128, 896),

time: 144 us -> 135 us (0.938)
  Pallas kernels: 136 us -> 131 us
  other arithmetic: 1.69 us -> 0 us
    pallas_call x1, Pallas kernels: 136 us -> 131 us  [body(): pl.pallas_call(kernel, out_shape=(jax.ShapeDtypeStruct((512, 512), BF), j...]
    another operation x1 -> x0, other arithmetic: 1.69 us -> none  [body(): jnp.stack([keys, values])]
where the time goes in v3:
time: 135 us
  Pallas kernels  131 us (97%)
  local copies, waits for them, and re-layouts  3.33 us (2%)
    pallas_call x1, Pallas kernels, body(): pl.pallas_call(kernel, out_shape=(jax.ShapeDtypeStruct((512, 512), BF), j...  131 us
    unnamed x7, local copies, waits for them, and re-layouts  3.33 us

profile of v3, /device:TPU:1, one launch (start us, length us, event | category | flops | bytes accessed | tf_op | source)
XLA Modules:
  0.0 134.6 jit_solution(8042067219692479209)
XLA Ops:
  0.6 130.6 %layer.1 = (bf16[512,512]{1,0:T(8,128)(2,1)}, f32[4,512]{1,0:T(4,128)}, bf16[512,512]{1,0:T(8,128)(2,1)}) custom-call(s32[16]{0:T(128)} %span_ref.1, f32[4096]{0:T(1024)} %gain_ref.1, bf16[512,512]{1,0:T(8,128)(2,1)} %q_in.1, bf16[512,128]{1,0:T(8,128)(2,1)} %k_in.1, bf16[512,128]{1,0:T(8,128)(2,1)} %v_in.1, bf16[512,512]{1,0:T(8,128)(2,1)} %f_in.1, ...), custom_call_target="tpu_custom_call" | custom-call | tf_op jit(solution)/shard_map/layer/pallas_call | solution.py:581
  131.2 0.0 copy-start.1
  131.3 0.0 copy-start
  131.3 1.9 %copy.15 = bf16[512,512]{1,0:T(8,128)(2,1)} copy(bf16[512,512]{1,0:T(8,128)(2,1)} %get-tuple-element.6) | data formatting | bytes 1048576
  133.2 0.0 copy-done.1
  133.2 0.6 copy.16
  133.8 0.0 copy-done
  133.8 0.8 copy.17
Async XLA Ops:
  131.2 1.9 %copy-start.1 = (f32[4,512]{1,0:T(4,128)S(1)}, f32[4,512]{1,0:T(4,128)}, u32[]{:S(2)}) copy-start(f32[4,512]{1,0:T(4,128)} %get-tuple-element.7) | copy-start | bytes 24580
  131.3 2.5 %copy-start = (bf16[512,512]{1,0:T(8,128)(2,1)S(1)}, bf16[512,512]{1,0:T(8,128)(2,1)}, u32[]{:S(2)}) copy-start(bf16[512,512]{1,0:T(8,128)(2,1)} %get-tuple-element.8) | copy-start | bytes 1572868

commit v4 on v3

--- a/solution.py
+++ b/solution.py
@@ -18,15 +18,16 @@
 SCALE2 = LOG2E / math.sqrt(HD)
 
 ORDER = (
-    "st", "K0", "F0a", "G0", "U0", "K4", "G1", "G2", "Fs", "F1a", "U4", "K8", "Kr0", "G3", "U1",
-    "U2", "Q", "Gr0", "U8", "G4", "F2a", "F0b", "U5", "G5", "G6", "U6", "Gr1", "U3", "U9", "Gr2",
-    "D0", "F2b", "F1b", "U10", "Ur1", "A00", "A01", "U7", "A02", "Ur2", "G7", "A03", "D2", "F3",
-    "Ur0", "K1", "N", "D1", "Gr3", "PU0", "PU2", "K5", "K2", "PU1", "U11", "PG0", "PG3", "PG1",
-    "K6", "D3", "Ur3", "PU3", "PG2", "K3", "D4", "ACT", "Dr0", "W02", "W01", "K9", "W03", "W00",
-    "D5", "D6", "K7", "Kr1", "A10", "X01", "X00", "K10", "A11", "Dr1", "W10", "W11", "W12", "A12",
-    "Dr2", "W21", "W23", "Kr2", "C0", "K11", "W20", "W22", "A13", "D7", "A20", "X10", "E0", "X11",
-    "Kr3", "A21", "A22", "Dr3", "W33", "W32", "W30", "A23", "X21", "X20", "A30", "W13", "C1", "A31",
-    "X30", "W31", "X31", "A32", "A33", "E1", "AF", "C2", "C3", "E2", "E3",
+    "st", "K0", "K12", "U0", "U12", "G0", "Fs", "F0a", "K4", "G2", "K1", "F1a", "U1", "U13", "U2",
+    "F2a", "G1", "U14", "U4", "K2", "F0b", "Qs", "U5", "G3", "K8", "Kr0", "U8", "U3", "U6", "D0",
+    "Ur0", "F1b", "F2b", "Q", "G4", "U15", "A00", "G5", "G6", "U9", "A01", "A02", "F3", "G8", "K3",
+    "N", "A03", "Gr1", "U7", "U10", "D2", "K13", "Gr0", "PG0", "PG1", "PU0", "Ur2", "K5", "D1",
+    "G7", "K15", "PU2", "Gr2", "K14", "U11", "Ur1", "PG2", "PU1", "Gr3", "PG3", "D3", "Ur3", "PU3",
+    "ACT", "Dr0", "W02", "W00", "D4", "W03", "K9", "K6", "W01", "D6", "D5", "K7", "D8", "X01",
+    "X00", "Kr1", "A10", "A11", "Dr1", "W12", "W10", "A12", "K10", "Dr2", "W11", "W22", "A13",
+    "X10", "W20", "Kr2", "D7", "K11", "A20", "X11", "A21", "W13", "Dr3", "W21", "X21", "X20", "W23",
+    "Kr3", "W32", "C0", "C1", "W31", "A22", "A23", "A30", "W30", "C2", "A31", "X30", "X31", "A32",
+    "A33", "AF", "E0", "W33", "C3", "E1", "E2", "E3",
 )
 
 
@@ -147,11 +148,17 @@
         for idx in idxs:
             copy_of(a, idx).wait_recv()
 
+    def first(a, mine, other):
+        local_of(a).wait()
+        pl.when(is_same)(lambda: go(a, *mine))
+        pl.when(not_same)(lambda: go(a, *other))
+        got(a, 0)
+        pl.when(is_same)(lambda: go(a, *other))
+        pl.when(not_same)(lambda: go(a, *mine))
+
     def ev_z(a, n):
         if n == 0:
-            local_of(a).wait()
-            got(a, 0)
-            go(a, 1, 2, 4, 8)
+            first(a, (1, 4, 8), (2,))
         elif n == 1:
             got(a, 1)
             go(a, 5, 9)
@@ -170,6 +177,7 @@
         elif n == 6:
             got(a, 6, 7)
             go(a, 15)
+        elif n == 8:
             got(a, 8, 9)
             go(a, 16)
         elif n == 7:
@@ -180,21 +188,20 @@
 
     def ev_y(a, n):
         if n == 0:
-            local_of(a).wait()
-            got(a, 0)
-            go(a, 4, 7, 5, 6, 20, 24)
+            first(a, (4, 6), (5, 7))
         elif n == 1:
             got(a, 4, 5)
-            go(a, 8, 21, 25)
+            go(a, 8)
         elif n == 2:
             got(a, 6, 7)
-            go(a, 9, 22, 26)
+            go(a, 9)
         elif n == 3:
             got(a, 8, 9)
-            go(a, 23, 27)
         elif n < 8:
             got(a, 20 + n)
             go(a, 24 + n)
+        elif n >= 12:
+            go(a, 8 + n, 12 + n)
         else:
             got(a, 12 + n, 20 + n)
             go(a, 6 + n)
@@ -251,12 +258,10 @@
         @pl.when(is_same)
         def _():
             f_loc.start()
-            q_loc.start()
 
         @pl.when(not_same)
         def _():
             xc(0).start()
-            xc(3).start()
 
         for half in range(2):
             @pl.when(c == half)
@@ -475,6 +480,9 @@
             start()
         elif nm[0] == "F":
             feat(nm)
+        elif nm == "Qs":
+            pl.when(is_same)(lambda: q_loc.start())
+            pl.when(not_same)(lambda: xc(3).start())
         elif nm == "Q":
             q_wait()
         elif nm == "AF":
@@ -573,18 +581,25 @@
             xc(it).wait_send()
 
 
+def move(a_in, l_in, f_in, a_out, l_out, f_out):
+    a_out[...] = a_in[...]
+    l_out[...] = l_in[...]
+    f_out[...] = f_in[...]
+
+
 def body(queries, keys, values, span_order, ffn_input, norm_gain, gate_w, up_w, down_w):
     anyspace = pl.BlockSpec(memory_space=pl.ANY)
     vmem = pl.BlockSpec(memory_space=pltpu.VMEM)
     smem = pl.BlockSpec(memory_space=pltpu.SMEM)
     sem = pltpu.SemaphoreType.DMA
-    return pl.pallas_call(
+    shapes = (
+        jax.ShapeDtypeStruct((512, 512), BF),
+        jax.ShapeDtypeStruct((4, 512), F32),
+        jax.ShapeDtypeStruct((512, 512), BF),
+    )
+    outs = pl.pallas_call(
         kernel,
-        out_shape=(
-            jax.ShapeDtypeStruct((512, 512), BF),
-            jax.ShapeDtypeStruct((4, 512), F32),
-            jax.ShapeDtypeStruct((512, 512), BF),
-        ),
+        out_shape=shapes,
         in_specs=[smem, vmem] + [anyspace] * 7,
         out_specs=(vmem, vmem, vmem),
         scratch_shapes=[
@@ -632,6 +647,13 @@
         up_w.reshape(2, 128, 896),
         down_w.reshape(2, 448, 256),
     )
+    return pl.pallas_call(
+        move,
+        out_shape=shapes,
+        in_specs=[vmem] * 3,
+        out_specs=(vmem,) * 3,
+        name="move",
+    )(*outs)
 
 
 def solution(mesh):

time: 135 us -> 132 us (0.978)
  local copies, waits for them, and re-layouts: 3.33 us -> 0 us
    unnamed x7 -> x0, local copies, waits for them, and re-layouts: 3.33 us -> none
    pallas_call x1 -> x2, Pallas kernels: 131 us -> 131 us  [the longest x1 128 us: body(): pl.pallas_call(kernel, out_shape=shapes, in_specs=[smem, vmem] + [anyspac...]
where the time goes in v4:
time: 132 us; the launch traced here: 131 us
  Pallas kernels  131 us (99%)
    pallas_call x1, Pallas kernels, body(): pl.pallas_call(kernel, out_shape=shapes, in_specs=[smem, vmem] + [anyspac...  128 us

profile of v4, /device:TPU:1, one launch (start us, length us, event | category | flops | bytes accessed | tf_op | source)
XLA Modules:
  0.0 131.3 jit_solution(16142473008475416305)
XLA Ops:
  0.6 128.5 %layer.1 = (bf16[512,512]{1,0:T(8,128)(2,1)}, f32[4,512]{1,0:T(4,128)}, bf16[512,512]{1,0:T(8,128)(2,1)}) custom-call(s32[16]{0:T(128)} %span_ref.1, f32[4096]{0:T(1024)} %gain_ref.1, bf16[512,512]{1,0:T(8,128)(2,1)} %q_in.1, bf16[512,128]{1,0:T(8,128)(2,1)} %k_in.1, bf16[512,128]{1,0:T(8,128)(2,1)} %v_in.1, bf16[512,512]{1,0:T(8,128)(2,1)} %f_in.1, ...), custom_call_target="tpu_custom_call" | custom-call | tf_op jit(solution)/shard_map/layer/pallas_call | solution.py:600
  129.1 2.2 %move.1 = (bf16[512,512]{1,0:T(8,128)(2,1)}, f32[4,512]{1,0:T(4,128)}, bf16[512,512]{1,0:T(8,128)(2,1)}) custom-call(bf16[512,512]{1,0:T(8,128)(2,1)} %get-tuple-element.6.a_in, f32[4,512]{1,0:T(4,128)} %get-tuple-element.7.l_in, bf16[512,512]{1,0:T(8,128)(2,1)} %get-tuple-element.8.f_in), custom_call_target="tpu_custom_call" | custom-call | tf_op jit(solution)/shard_map/move/pallas_call | solution.py:650

commit v5 on v4

--- a/solution.py
+++ b/solution.py
@@ -208,6 +208,7 @@
 
     k0 = 2 * x + c
     two = pl.ds(2 * x, 2)
+    left, right = pl.ds(0, 128), pl.ds(128, 128)
 
     def out_copy(g):
         return remote(o_b.at[g], orx_b.at[g], xs_sem.at[42 + g], xr_sem.at[42 + g], OPPD)
@@ -232,13 +233,18 @@
             return cp(f_b.at[2 * xr + 1], f_b.at[2 * xr + 1], XL)
         if i == 9:
             return cp(lg_b, lrx_b, OPPD)
-        if i < 14:
-            n = i - 10
-            return cp(r_b.at[n], rx_b.at[n], {"ctx": yo * 4 + z, "kvh": 2 * x + groups[n] // 2})
+        if i < 14 or i >= 54:
+            n, cols = (i - 10, left) if i < 14 else (i - 54, right)
+            core = {"ctx": yo * 4 + z, "kvh": 2 * x + groups[n] // 2}
+            return cp(r_b.at[n, :, cols], rx_b.at[n, :, cols], core)
         if i < 18:
             return cp(r_b.at[i - 14], fo_b.at[i - 14], SIB)
         g, n = (i - 18) // 6, (i - 18) % 6
         lo, hi = pl.ds(0, 256), pl.ds(256, 256)
+        if i >= 46:
+            g, n = (i - 46) // 2, (i - 46) % 2
+            rows = hi if n else lo
+            return cp(ps_b.at[g, n, rows, right], rs_b.at[g, n, rows, right], XL if n else XR)
         if n == 0:
             return cp(ps_b.at[g, 2, lo], fr_b.at[g, 0], XR)
         if n == 1:
@@ -248,8 +254,8 @@
         if n == 3:
             return cp(ps_b.at[g, 1, lo], rs_b.at[g, 1, lo], XL)
         if n == 4:
-            return cp(ps_b.at[g, 0, lo], rs_b.at[g, 0, lo], XR)
-        return cp(ps_b.at[g, 1, hi], rs_b.at[g, 1, hi], XL)
+            return cp(ps_b.at[g, 0, lo, left], rs_b.at[g, 0, lo, left], XR)
+        return cp(ps_b.at[g, 1, hi, left], rs_b.at[g, 1, hi, left], XL)
 
     f_loc = pltpu.make_async_copy(f_in, f_b.at[k0], loc_sem.at[4])
     q_loc = pltpu.make_async_copy(q_in, q_b, loc_sem.at[5])
@@ -442,15 +448,23 @@
         rows = pl.ds(256 * n, 256)
         ps_b[i, n, rows] = (ps_b[i, n, rows].astype(F32) + fr_b[i, n].astype(F32)).astype(BF)
         x_go(i, 4 + n)
+        xc(46 + 2 * i + n).start()
+        sent[46 + 2 * i + n] = True
 
     def combine(i):
-        x_got(i, 2, 3, 4, 5)
-        total = po_b[i] + rs_b[i, 0].astype(F32) + rs_b[i, 1].astype(F32)
-        r_b[i] = total.astype(BF)
-
-        @pl.when(not_same)
-        def _():
-            xc(10 + i).start()
+        x_got(i, 2, 3)
+        for m, cols in enumerate((left, right)):
+            if m == 0:
+                x_got(i, 4, 5)
+            else:
+                xc(46 + 2 * i).wait_recv()
+                xc(47 + 2 * i).wait_recv()
+            total = po_b[i, :, cols] + rs_b[i, 0, :, cols].astype(F32)
+            r_b[i, :, cols] = (total + rs_b[i, 1, :, cols].astype(F32)).astype(BF)
+
+            @pl.when(not_same)
+            def _():
+                xc(10 + i + 44 * m).start()
 
         @pl.when(is_same & (groups[i] // 2 != c))
         def _():
@@ -458,22 +472,23 @@
 
     def close(i):
         zs = groups[i]
-        off = pl.multiple_of((zs % 2) * 256, 256)
 
         @pl.when(zs // 2 == c)
         def _():
-            xc(10 + i).wait_recv()
-
-            @pl.when(is_same)
-            def _():
-                res = r_b[i].astype(F32) + rx_b[i].astype(F32)
-                ffn_out[:, pl.ds(off, 256)] = res.astype(BF)
-
-            @pl.when(not_same)
-            def _():
-                xc(14 + i).wait_recv()
-                res = fo_b[i].astype(F32) + rx_b[i].astype(F32)
-                ffn_out[:, pl.ds(off, 256)] = res.astype(BF)
+            pl.when(not_same)(lambda: xc(14 + i).wait_recv())
+            for m, cols in enumerate((left, right)):
+                xc(10 + i + 44 * m).wait_recv()
+                out = pl.ds(pl.multiple_of((zs % 2) * 256 + 128 * m, 128), 128)
+
+                @pl.when(is_same)
+                def _():
+                    res = r_b[i, :, cols].astype(F32) + rx_b[i, :, cols].astype(F32)
+                    ffn_out[:, out] = res.astype(BF)
+
+                @pl.when(not_same)
+                def _():
+                    res = fo_b[i, :, cols].astype(F32) + rx_b[i, :, cols].astype(F32)
+                    ffn_out[:, out] = res.astype(BF)
 
     def run(nm):
         if nm == "st":
@@ -571,6 +586,7 @@
             att_out[:, g * HD : g * HD + HD] = orx_b[g]
         for i in range(4):
             xc(10 + i).wait_send()
+            xc(54 + i).wait_send()
 
     for i in (4, 5, 6, 7):
         xc(i).wait_send()
@@ -629,8 +645,8 @@
             sem((6,)),
             sem((4, 32)),
             sem((4, 32)),
-            sem((46,)),
-            sem((46,)),
+            sem((58,)),
+            sem((58,)),
         ],
         compiler_params=pltpu.CompilerParams(
             collective_id=0, has_side_effects=True, vmem_limit_bytes=63 * 2**20

time: 132 us -> 132 us (level)
  no operation moved by 1% of the time
where the time goes in v5:
time: 132 us; the launch traced here: 131 us
  Pallas kernels  131 us (99%)
    pallas_call x1, Pallas kernels, body(): pl.pallas_call(kernel, out_shape=shapes, in_specs=[smem, vmem] + [anyspac...  129 us

profile of v5, /device:TPU:1, one launch (start us, length us, event | category | flops | bytes accessed | tf_op | source)
XLA Modules:
  0.0 131.4 jit_solution(453688814861597986)
XLA Ops:
  0.6 128.6 %layer.1 = (bf16[512,512]{1,0:T(8,128)(2,1)}, f32[4,512]{1,0:T(4,128)}, bf16[512,512]{1,0:T(8,128)(2,1)}) custom-call(s32[16]{0:T(128)} %span_ref.1, f32[4096]{0:T(1024)} %gain_ref.1, bf16[512,512]{1,0:T(8,128)(2,1)} %q_in.1, bf16[512,128]{1,0:T(8,128)(2,1)} %k_in.1, bf16[512,128]{1,0:T(8,128)(2,1)} %v_in.1, bf16[512,512]{1,0:T(8,128)(2,1)} %f_in.1, ...), custom_call_target="tpu_custom_call" | custom-call | tf_op jit(solution)/shard_map/layer/pallas_call | solution.py:616
  129.2 2.2 %move.1 = (bf16[512,512]{1,0:T(8,128)(2,1)}, f32[4,512]{1,0:T(4,128)}, bf16[512,512]{1,0:T(8,128)(2,1)}) custom-call(bf16[512,512]{1,0:T(8,128)(2,1)} %get-tuple-element.6.a_in, f32[4,512]{1,0:T(4,128)} %get-tuple-element.7.l_in, bf16[512,512]{1,0:T(8,128)(2,1)} %get-tuple-element.8.f_in), custom_call_target="tpu_custom_call" | custom-call | tf_op jit(solution)/shard_map/move/pallas_call | solution.py:666
